TPU v7x, 512 devices: a whole 4x8x8 slice. The times are simulated.
512 devices in a mesh: gx: 128 (over z, y_hi, x, core), gy: 4 (over y_lo).
Axes of the slice: x: 4, y: 8 (y_hi: 2, y_lo: 4; y = y_hi * 4 + y_lo), z: 8, core: 2. Of those that a mesh axis runs over, the one named last changes fastest.
Arguments:
- sensitivity: float32 [7, 2048, 128, 128], P(None, 'gx', 'gy'), may hold values from -6 to 6
- velocity: float32 [3, 2048, 128, 128], P(None, 'gx', 'gy'), may hold values from -0.1 to 0.1
- omega: float32 [2048, 128, 128], P('gx', 'gy'), may hold values from 0.8 to 1.8
- solid: int32 [2048, 128, 128], P('gx', 'gy'), may hold values 0 or 1
- active: int32 [128, 8, 8], P('gx', 'gy'), may hold values 0 or 1
Outputs:
- adjoint: float32 [7, 2048, 128, 128], P(None, 'gx', 'gy')
All inputs are finite; a program needn't handle non-finite values. No bound on the sum of `solid` or of `active` on one device may be relied on, other than what follows from the above.
Results may differ from a plain program's by a relative error of at most 0.00002.
Values sent between devices are 32-bit elements; how exact they have to be, the bound alone decides.
No kernel may reach another device: no remote copies, remote signals or barrier semaphores. Data moves between devices by JAX's collectives and lax.ppermute only.
A program may use at most 64 MiB of HBM per device.

v0:
```python
import jax
import jax.numpy as jnp
from jax import lax
from jax.sharding import PartitionSpec as P

BLOCK = 16
ITERS = 4


moves = ((0, 0, 0), (1, 0, 0), (-1, 0, 0), (0, 1, 0), (0, -1, 0), (0, 0, 1), (0, 0, -1))
opposite = (0, 2, 1, 4, 3, 6, 5)
weights = (0.25, 0.125, 0.125, 0.125, 0.125, 0.125, 0.125)


def extended(block, sides, width):
    for axis, dim in sides:
        count = lax.axis_size(axis)
        forward = [(i, i + 1) for i in range(count - 1)]
        backward = [(target, source) for source, target in forward]
        low = lax.ppermute(
            lax.slice_in_dim(block, block.shape[dim] - width, None, axis=dim), axis, forward
        )
        high = lax.ppermute(lax.slice_in_dim(block, 0, width, axis=dim), axis, backward)
        block = jnp.concatenate([low, block, high], axis=dim)
    return block


def adjoint_core(g_ext, stat_ext):
    width_a = g_ext.shape[1] - 2
    width_b = g_ext.shape[2] - 2
    depth_z = g_ext.shape[3]
    padded = jnp.pad(g_ext, ((0, 0), (0, 0), (0, 0), (1, 1)))
    flags = jnp.pad(stat_ext[0], ((0, 0), (0, 0), (1, 1)))
    centre = padded[:, 1:-1, 1:-1, 1:-1]
    fluid = flags[1:-1, 1:-1, 1:-1]
    inner = stat_ext[:, 1:-1, 1:-1, :]
    speed_x, speed_y, speed_z, rate = (inner[1], inner[2], inner[3], inner[4])
    pulled = []
    total = jnp.zeros_like(fluid)
    for index in range(7):
        step_x, step_y, step_z = moves[index]
        near = padded[
            index,
            1 + step_x : 1 + step_x + width_a,
            1 + step_y : 1 + step_y + width_b,
            1 + step_z : 1 + step_z + depth_z,
        ]
        near_flag = flags[
            1 + step_x : 1 + step_x + width_a,
            1 + step_y : 1 + step_y + width_b,
            1 + step_z : 1 + step_z + depth_z,
        ]
        pulled_one = near_flag * near + (1.0 - near_flag) * centre[opposite[index]]
        weight = weights[index] * (
            1.0 + 4.0 * (step_x * speed_x + step_y * speed_y + step_z * speed_z)
        )
        total = total + weight * pulled_one
        pulled.append(pulled_one)
    result = [fluid * ((1.0 - rate) * pulled[index] + rate * total) for index in range(7)]
    return jnp.stack(result)


def extend(field, reach):
    return extended(field, (("gx", 1), ("gy", 2)), reach)


def on_device(sensitivity, velocity, omega, solid, active):
    expanded = jnp.repeat(
        jnp.repeat(jnp.repeat(active, BLOCK, axis=0), BLOCK, axis=1), BLOCK, axis=2
    )
    fluid = (1 - solid).astype(jnp.float32) * expanded.astype(jnp.float32)
    field = sensitivity
    flag_ext = extended(fluid[None], (("gx", 1), ("gy", 2)), 1)
    rest = jnp.stack([velocity[0], velocity[1], velocity[2], omega])
    rest_ext = jnp.pad(rest, ((0, 0), (1, 1), (1, 1), (0, 0)))
    static_ext = jnp.concatenate([flag_ext, rest_ext], axis=0)
    for step in range(ITERS):
        field = adjoint_core(extend(field, 1), static_ext)
    return field


def solution(mesh):
    in_specs = (
        P(None, "gx", "gy", None),
        P(None, "gx", "gy", None),
        P("gx", "gy", None),
        P("gx", "gy", None),
        P("gx", "gy", None),
    )
    out_specs = P(None, "gx", "gy", None)
    return jax.shard_map(
        on_device, mesh=mesh, in_specs=in_specs, out_specs=out_specs, check_vma=False
    )
```

profile of v0, /device:TPU:231, one launch (start us, length us, event | category | flops | bytes accessed | tf_op | source)
XLA Modules:
  0.0 152.7 jit_solution(12872964060556281021)
XLA Ops:
  2.0 5.2 %collective-permute-start = (f32[1,1,32,128]{3,2,1,0:T(8,128)S(1)}, f32[1,1,32,128]{3,2,1,0:T(8,128)S(1)}, u32[]{:S(2)}, u32[]{:S(2)}) collective-permute-start(f32[1,1,32,128]{3,2,1,0:T(8,128)S(1)} %get-tuple-element.80), channel_id=1, source_target_pairs={{0,4},{4,8},{8,12},{12,16},{16,20},{20,24},{24,28},{28,32},{32,36}... | collective-permute-start | bytes 49160 | tf_op jit(solution)/shard_map/ppermute | solution.py:20
  10.2 11.8 %collective-permute-start.5 = (f32[7,1,32,128]{3,2,1,0:T(8,128)S(1)}, f32[7,1,32,128]{3,2,1,0:T(8,128)S(1)}, u32[]{:S(2)}, u32[]{:S(2)}) collective-permute-start(f32[7,1,32,128]{3,2,1,0:T(8,128)S(1)} %get-tuple-element.76), channel_id=1, source_target_pairs={{0,4},{4,8},{8,12},{12,16},{16,20},{20,24},{24,28},{28,32},{32,36}... | collective-permute-start | bytes 344072 | tf_op jit(solution)/shard_map/ppermute | solution.py:20
  23.9 3.2 %collective-permute-start.2 = (f32[1,18,1,128]{3,2,1,0:T(1,128)S(1)}, f32[1,18,1,128]{3,2,1,0:T(1,128)S(1)}, u32[]{:S(2)}, u32[]{:S(2)}) collective-permute-start(f32[1,18,1,128]{3,2,1,0:T(1,128)S(1)} %get-tuple-element.78), channel_id=1, source_target_pairs={{0,1},{1,2},{2,3},{4,5},{5,6},{6,7},{8,9},{9,10},{10,11},{12,13},{... | collective-permute-start | bytes 27656 | tf_op jit(solution)/shard_map/ppermute | solution.py:20
  30.1 7.4 %collective-permute-done.4 = f32[7,1,32,128]{3,2,1,0:T(8,128)S(1)} collective-permute-done((f32[7,1,32,128]{3,2,1,0:T(8,128)S(1)}, f32[7,1,32,128]{3,2,1,0:T(8,128)S(1)}, u32[]{:S(2)}, u32[]{:S(2)}) %collective-permute-start.4) | collective-permute-done | bytes 114720 | tf_op jit(solution)/shard_map/ppermute | solution.py:23
  37.7 1.9 %collective-permute-start.7 = (f32[7,18,1,128]{3,2,1,0:T(1,128)S(1)}, f32[7,18,1,128]{3,2,1,0:T(1,128)S(1)}, u32[]{:S(2)}, u32[]{:S(2)}) collective-permute-start(f32[7,18,1,128]{3,2,1,0:T(1,128)S(1)} %get-tuple-element.68), channel_id=1, source_target_pairs={{0,1},{1,2},{2,3},{4,5},{5,6},{6,7},{8,9},{9,10},{10,11},{12,13},{... | collective-permute-start | bytes 193544 | tf_op jit(solution)/shard_map/ppermute | solution.py:20
  41.0 5.2 %collective-permute-done.6 = f32[7,18,1,128]{3,2,1,0:T(1,128)S(1)} collective-permute-done((f32[7,18,1,128]{3,2,1,0:T(1,128)S(1)}, f32[7,18,1,128]{3,2,1,0:T(1,128)S(1)}, u32[]{:S(2)}, u32[]{:S(2)}) %collective-permute-start.6) | collective-permute-done | bytes 64544 | tf_op jit(solution)/shard_map/ppermute | solution.py:23
  46.2 2.6 %select_maximum_fusion.12 = f32[7,18,34,130]{3,2,1,0:T(8,128)S(1)} fusion(f32[7,18,1,128]{3,2,1,0:T(1,128)S(1)} %collective-permute-done.6, f32[7,18,32,128]{3,2,1,0:T(8,128)S(1)} %constant_dynamic-update-slice_fusion, f32[7,18,1,128]{3,2,1,0:T(1,128)S(1)} %collective-permute-done.7), kind=kLoop, calls=%fused_computation.14 | loop fusion | flops 4455360 | bytes 4421088 | tf_op jit(solution)/shard_map/concatenate | solution.py:24
  50.4 6.8 %collective-permute-start.9 = (f32[7,1,32,128]{3,2,1,0:T(8,128)S(1)}, f32[7,1,32,128]{3,2,1,0:T(8,128)S(1)}, u32[]{:S(2)}, u32[]{:S(2)}) collective-permute-start(f32[7,1,32,128]{3,2,1,0:T(8,128)S(1)} %get-tuple-element.74), channel_id=1, source_target_pairs={{0,4},{4,8},{8,12},{12,16},{16,20},{20,24},{24,28},{28,32},{32,36}... | collective-permute-start | bytes 344072 | tf_op jit(solution)/shard_map/ppermute | solution.py:20
  57.2 1.9 %collective-permute-start.8 = (f32[7,1,32,128]{3,2,1,0:T(8,128)S(1)}, f32[7,1,32,128]{3,2,1,0:T(8,128)S(1)}, u32[]{:S(2)}, u32[]{:S(2)}) collective-permute-start(f32[7,1,32,128]{3,2,1,0:T(8,128)S(1)} %get-tuple-element.75), channel_id=1, source_target_pairs={{4,0},{8,4},{12,8},{16,12},{20,16},{24,20},{28,24},{32,28},{36,32}... | collective-permute-start | bytes 344072 | tf_op jit(solution)/shard_map/ppermute | solution.py:23
  59.2 12.4 %collective-permute-done.8 = f32[7,1,32,128]{3,2,1,0:T(8,128)S(1)} collective-permute-done((f32[7,1,32,128]{3,2,1,0:T(8,128)S(1)}, f32[7,1,32,128]{3,2,1,0:T(8,128)S(1)}, u32[]{:S(2)}, u32[]{:S(2)}) %collective-permute-start.8) | collective-permute-done | bytes 114720 | tf_op jit(solution)/shard_map/ppermute | solution.py:23
  71.6 4.3 %collective-permute-start.11 = (f32[7,18,1,128]{3,2,1,0:T(1,128)S(1)}, f32[7,18,1,128]{3,2,1,0:T(1,128)S(1)}, u32[]{:S(2)}, u32[]{:S(2)}) collective-permute-start(f32[7,18,1,128]{3,2,1,0:T(1,128)S(1)} %get-tuple-element.66), channel_id=1, source_target_pairs={{0,1},{1,2},{2,3},{4,5},{5,6},{6,7},{8,9},{9,10},{10,11},{12,13},{... | collective-permute-start | bytes 193544 | tf_op jit(solution)/shard_map/ppermute | solution.py:20
  77.3 4.0 %collective-permute-done.10 = f32[7,18,1,128]{3,2,1,0:T(1,128)S(1)} collective-permute-done((f32[7,18,1,128]{3,2,1,0:T(1,128)S(1)}, f32[7,18,1,128]{3,2,1,0:T(1,128)S(1)}, u32[]{:S(2)}, u32[]{:S(2)}) %collective-permute-start.10) | collective-permute-done | bytes 64544 | tf_op jit(solution)/shard_map/ppermute | solution.py:23
  81.3 4.5 %select_maximum_fusion.8 = f32[7,18,34,130]{3,2,1,0:T(8,128)S(1)} fusion(f32[7,18,1,128]{3,2,1,0:T(1,128)S(1)} %collective-permute-done.10, f32[7,18,1,128]{3,2,1,0:T(1,128)S(1)} %collective-permute-done.11, f32[7,1,32,128]{3,2,1,0:T(8,128)S(1)} %collective-permute-done.8, f32[7,16,32,128]{3,2,1,0:T(8,128)S(1)} %bitcast_dynamic-update-slice_fusion.21, ...), kind=kLoop, calls=%fused_computation.10 | loop fusion | flops 6683040 | bytes 4421088 | tf_op jit(solution)/shard_map/concatenate | solution.py:24
  87.7 2.9 %collective-permute-start.13 = (f32[7,1,32,128]{3,2,1,0:T(8,128)S(1)}, f32[7,1,32,128]{3,2,1,0:T(8,128)S(1)}, u32[]{:S(2)}, u32[]{:S(2)}) collective-permute-start(f32[7,1,32,128]{3,2,1,0:T(8,128)S(1)} %get-tuple-element.72), channel_id=1, source_target_pairs={{0,4},{4,8},{8,12},{12,16},{16,20},{20,24},{24,28},{28,32},{32,36}... | collective-permute-start | bytes 344072 | tf_op jit(solution)/shard_map/ppermute | solution.py:20
  90.6 1.9 %collective-permute-start.12 = (f32[7,1,32,128]{3,2,1,0:T(8,128)S(1)}, f32[7,1,32,128]{3,2,1,0:T(8,128)S(1)}, u32[]{:S(2)}, u32[]{:S(2)}) collective-permute-start(f32[7,1,32,128]{3,2,1,0:T(8,128)S(1)} %get-tuple-element.73), channel_id=1, source_target_pairs={{4,0},{8,4},{12,8},{16,12},{20,16},{24,20},{28,24},{32,28},{36,32}... | collective-permute-start | bytes 344072 | tf_op jit(solution)/shard_map/ppermute | solution.py:23
  92.5 12.3 %collective-permute-done.12 = f32[7,1,32,128]{3,2,1,0:T(8,128)S(1)} collective-permute-done((f32[7,1,32,128]{3,2,1,0:T(8,128)S(1)}, f32[7,1,32,128]{3,2,1,0:T(8,128)S(1)}, u32[]{:S(2)}, u32[]{:S(2)}) %collective-permute-start.12) | collective-permute-done | bytes 114720 | tf_op jit(solution)/shard_map/ppermute | solution.py:23
  104.9 3.0 %collective-permute-start.15 = (f32[7,18,1,128]{3,2,1,0:T(1,128)S(1)}, f32[7,18,1,128]{3,2,1,0:T(1,128)S(1)}, u32[]{:S(2)}, u32[]{:S(2)}) collective-permute-start(f32[7,18,1,128]{3,2,1,0:T(1,128)S(1)} %get-tuple-element.64), channel_id=1, source_target_pairs={{0,1},{1,2},{2,3},{4,5},{5,6},{6,7},{8,9},{9,10},{10,11},{12,13},{... | collective-permute-start | bytes 193544 | tf_op jit(solution)/shard_map/ppermute | solution.py:20
  109.2 3.7 %collective-permute-done.14 = f32[7,18,1,128]{3,2,1,0:T(1,128)S(1)} collective-permute-done((f32[7,18,1,128]{3,2,1,0:T(1,128)S(1)}, f32[7,18,1,128]{3,2,1,0:T(1,128)S(1)}, u32[]{:S(2)}, u32[]{:S(2)}) %collective-permute-start.14) | collective-permute-done | bytes 64544 | tf_op jit(solution)/shard_map/ppermute | solution.py:23
  112.9 4.5 %select_maximum_fusion.4 = f32[7,18,34,130]{3,2,1,0:T(8,128)S(1)} fusion(f32[7,18,1,128]{3,2,1,0:T(1,128)S(1)} %collective-permute-done.14, f32[7,18,1,128]{3,2,1,0:T(1,128)S(1)} %collective-permute-done.15, f32[7,1,32,128]{3,2,1,0:T(8,128)S(1)} %collective-permute-done.12, f32[7,16,32,128]{3,2,1,0:T(8,128)S(1)} %bitcast_dynamic-update-slice_fusion.14, ...), kind=kLoop, calls=%fused_computation.6 | loop fusion | flops 6683040 | bytes 4421088 | tf_op jit(solution)/shard_map/concatenate | solution.py:24
  119.6 3.2 %collective-permute-start.17 = (f32[7,1,32,128]{3,2,1,0:T(8,128)S(1)}, f32[7,1,32,128]{3,2,1,0:T(8,128)S(1)}, u32[]{:S(2)}, u32[]{:S(2)}) collective-permute-start(f32[7,1,32,128]{3,2,1,0:T(8,128)S(1)} %get-tuple-element.70), channel_id=1, source_target_pairs={{0,4},{4,8},{8,12},{12,16},{16,20},{20,24},{24,28},{28,32},{32,36}... | collective-permute-start | bytes 344072 | tf_op jit(solution)/shard_map/ppermute | solution.py:20
  122.8 2.1 %collective-permute-start.16 = (f32[7,1,32,128]{3,2,1,0:T(8,128)S(1)}, f32[7,1,32,128]{3,2,1,0:T(8,128)S(1)}, u32[]{:S(2)}, u32[]{:S(2)}) collective-permute-start(f32[7,1,32,128]{3,2,1,0:T(8,128)S(1)} %get-tuple-element.71), channel_id=1, source_target_pairs={{4,0},{8,4},{12,8},{16,12},{20,16},{24,20},{28,24},{32,28},{36,32}... | collective-permute-start | bytes 344072 | tf_op jit(solution)/shard_map/ppermute | solution.py:23
  125.0 12.1 %collective-permute-done.16 = f32[7,1,32,128]{3,2,1,0:T(8,128)S(1)} collective-permute-done((f32[7,1,32,128]{3,2,1,0:T(8,128)S(1)}, f32[7,1,32,128]{3,2,1,0:T(8,128)S(1)}, u32[]{:S(2)}, u32[]{:S(2)}) %collective-permute-start.16) | collective-permute-done | bytes 114720 | tf_op jit(solution)/shard_map/ppermute | solution.py:23
  140.1 3.7 %collective-permute-done.18 = f32[7,18,1,128]{3,2,1,0:T(1,128)S(1)} collective-permute-done((f32[7,18,1,128]{3,2,1,0:T(1,128)S(1)}, f32[7,18,1,128]{3,2,1,0:T(1,128)S(1)}, u32[]{:S(2)}, u32[]{:S(2)}) %collective-permute-start.18) | collective-permute-done | bytes 64544 | tf_op jit(solution)/shard_map/ppermute | solution.py:23
  143.8 4.5 %select_maximum_fusion = f32[7,18,34,130]{3,2,1,0:T(8,128)S(1)} fusion(f32[7,18,1,128]{3,2,1,0:T(1,128)S(1)} %collective-permute-done.18, f32[7,18,1,128]{3,2,1,0:T(1,128)S(1)} %collective-permute-done.19, f32[7,1,32,128]{3,2,1,0:T(8,128)S(1)} %collective-permute-done.16, f32[7,16,32,128]{3,2,1,0:T(8,128)S(1)} %bitcast_dynamic-update-slice_fusion.7, ...), kind=kLoop, calls=%fused_computation.2 | loop fusion | flops 6683040 | bytes 4421088 | tf_op jit(solution)/shard_map/concatenate | solution.py:24
  (77 shorter events, 27.0 us)
Async XLA Ops:
  2.0 21.9 %collective-permute-start = (f32[1,1,32,128]{3,2,1,0:T(8,128)S(1)}, f32[1,1,32,128]{3,2,1,0:T(8,128)S(1)}, u32[]{:S(2)}, u32[]{:S(2)}) collective-permute-start(f32[1,1,32,128]{3,2,1,0:T(8,128)S(1)} %get-tuple-element.80), channel_id=1, source_target_pairs={{0,4},{4,8},{8,12},{12,16},{16,20},{20,24},{24,28},{28,32},{32,36}... | collective-permute-start | bytes 49160 | tf_op jit(solution)/shard_map/ppermute | solution.py:20
  7.2 16.6 %collective-permute-start.1 = (f32[1,1,32,128]{3,2,1,0:T(8,128)S(1)}, f32[1,1,32,128]{3,2,1,0:T(8,128)S(1)}, u32[]{:S(2)}, u32[]{:S(2)}) collective-permute-start(f32[1,1,32,128]{3,2,1,0:T(8,128)S(1)} %get-tuple-element.81), channel_id=1, source_target_pairs={{4,0},{8,4},{12,8},{16,12},{20,16},{24,20},{28,24},{32,28},{36,32}... | collective-permute-start | bytes 49160 | tf_op jit(solution)/shard_map/ppermute | solution.py:23
  10.2 18.3 %collective-permute-start.5 = (f32[7,1,32,128]{3,2,1,0:T(8,128)S(1)}, f32[7,1,32,128]{3,2,1,0:T(8,128)S(1)}, u32[]{:S(2)}, u32[]{:S(2)}) collective-permute-start(f32[7,1,32,128]{3,2,1,0:T(8,128)S(1)} %get-tuple-element.76), channel_id=1, source_target_pairs={{0,4},{4,8},{8,12},{12,16},{16,20},{20,24},{24,28},{28,32},{32,36}... | collective-permute-start | bytes 344072 | tf_op jit(solution)/shard_map/ppermute | solution.py:20
  21.9 15.6 %collective-permute-start.4 = (f32[7,1,32,128]{3,2,1,0:T(8,128)S(1)}, f32[7,1,32,128]{3,2,1,0:T(8,128)S(1)}, u32[]{:S(2)}, u32[]{:S(2)}) collective-permute-start(f32[7,1,32,128]{3,2,1,0:T(8,128)S(1)} %get-tuple-element.77), channel_id=1, source_target_pairs={{4,0},{8,4},{12,8},{16,12},{20,16},{24,20},{28,24},{32,28},{36,32}... | collective-permute-start | bytes 344072 | tf_op jit(solution)/shard_map/ppermute | solution.py:23
  23.9 17.0 %collective-permute-start.2 = (f32[1,18,1,128]{3,2,1,0:T(1,128)S(1)}, f32[1,18,1,128]{3,2,1,0:T(1,128)S(1)}, u32[]{:S(2)}, u32[]{:S(2)}) collective-permute-start(f32[1,18,1,128]{3,2,1,0:T(1,128)S(1)} %get-tuple-element.78), channel_id=1, source_target_pairs={{0,1},{1,2},{2,3},{4,5},{5,6},{6,7},{8,9},{9,10},{10,11},{12,13},{... | collective-permute-start | bytes 27656 | tf_op jit(solution)/shard_map/ppermute | solution.py:20
  27.1 13.8 %collective-permute-start.3 = (f32[1,18,1,128]{3,2,1,0:T(1,128)S(1)}, f32[1,18,1,128]{3,2,1,0:T(1,128)S(1)}, u32[]{:S(2)}, u32[]{:S(2)}) collective-permute-start(f32[1,18,1,128]{3,2,1,0:T(1,128)S(1)} %get-tuple-element.79), channel_id=1, source_target_pairs={{1,0},{2,1},{3,2},{5,4},{6,5},{7,6},{9,8},{10,9},{11,10},{13,12},{... | collective-permute-start | bytes 27656 | tf_op jit(solution)/shard_map/ppermute | solution.py:23
  37.7 3.3 %collective-permute-start.7 = (f32[7,18,1,128]{3,2,1,0:T(1,128)S(1)}, f32[7,18,1,128]{3,2,1,0:T(1,128)S(1)}, u32[]{:S(2)}, u32[]{:S(2)}) collective-permute-start(f32[7,18,1,128]{3,2,1,0:T(1,128)S(1)} %get-tuple-element.68), channel_id=1, source_target_pairs={{0,1},{1,2},{2,3},{4,5},{5,6},{6,7},{8,9},{9,10},{10,11},{12,13},{... | collective-permute-start | bytes 193544 | tf_op jit(solution)/shard_map/ppermute | solution.py:20
  39.6 6.6 %collective-permute-start.6 = (f32[7,18,1,128]{3,2,1,0:T(1,128)S(1)}, f32[7,18,1,128]{3,2,1,0:T(1,128)S(1)}, u32[]{:S(2)}, u32[]{:S(2)}) collective-permute-start(f32[7,18,1,128]{3,2,1,0:T(1,128)S(1)} %get-tuple-element.69), channel_id=1, source_target_pairs={{1,0},{2,1},{3,2},{5,4},{6,5},{7,6},{9,8},{10,9},{11,10},{13,12},{... | collective-permute-start | bytes 193544 | tf_op jit(solution)/shard_map/ppermute | solution.py:23
  41.0 7.8 %copy-start = (f32[16,32,128]{2,1,0:T(8,128)S(1)}, f32[16,32,128]{2,1,0:T(8,128)}, u32[]{:S(2)}) copy-start(f32[16,32,128]{2,1,0:T(8,128)} %param.7) | copy-start | bytes 786436
  41.0 7.8 %copy-start.2 = (f32[3,16,32,128]{3,2,1,0:T(8,128)S(1)}, f32[3,16,32,128]{3,2,1,0:T(8,128)}, u32[]{:S(2)}) copy-start(f32[3,16,32,128]{3,2,1,0:T(8,128)} %param.6) | copy-start | bytes 2359300
  46.2 2.6 %copy-start.1 = (f32[7,16,32,128]{3,2,1,0:T(8,128)S(1)}, f32[7,16,32,128]{3,2,1,0:T(8,128)}, u32[]{:S(2)}) copy-start(f32[7,16,32,128]{3,2,1,0:T(8,128)} %param.5) | copy-start | bytes 5505028
  50.4 8.7 %collective-permute-start.9 = (f32[7,1,32,128]{3,2,1,0:T(8,128)S(1)}, f32[7,1,32,128]{3,2,1,0:T(8,128)S(1)}, u32[]{:S(2)}, u32[]{:S(2)}) collective-permute-start(f32[7,1,32,128]{3,2,1,0:T(8,128)S(1)} %get-tuple-element.74), channel_id=1, source_target_pairs={{0,4},{4,8},{8,12},{12,16},{16,20},{20,24},{24,28},{28,32},{32,36}... | collective-permute-start | bytes 344072 | tf_op jit(solution)/shard_map/ppermute | solution.py:20
  57.2 14.3 %collective-permute-start.8 = (f32[7,1,32,128]{3,2,1,0:T(8,128)S(1)}, f32[7,1,32,128]{3,2,1,0:T(8,128)S(1)}, u32[]{:S(2)}, u32[]{:S(2)}) collective-permute-start(f32[7,1,32,128]{3,2,1,0:T(8,128)S(1)} %get-tuple-element.75), channel_id=1, source_target_pairs={{4,0},{8,4},{12,8},{16,12},{20,16},{24,20},{28,24},{32,28},{36,32}... | collective-permute-start | bytes 344072 | tf_op jit(solution)/shard_map/ppermute | solution.py:23
  71.6 5.6 %collective-permute-start.11 = (f32[7,18,1,128]{3,2,1,0:T(1,128)S(1)}, f32[7,18,1,128]{3,2,1,0:T(1,128)S(1)}, u32[]{:S(2)}, u32[]{:S(2)}) collective-permute-start(f32[7,18,1,128]{3,2,1,0:T(1,128)S(1)} %get-tuple-element.66), channel_id=1, source_target_pairs={{0,1},{1,2},{2,3},{4,5},{5,6},{6,7},{8,9},{9,10},{10,11},{12,13},{... | collective-permute-start | bytes 193544 | tf_op jit(solution)/shard_map/ppermute | solution.py:20
  76.0 5.3 %collective-permute-start.10 = (f32[7,18,1,128]{3,2,1,0:T(1,128)S(1)}, f32[7,18,1,128]{3,2,1,0:T(1,128)S(1)}, u32[]{:S(2)}, u32[]{:S(2)}) collective-permute-start(f32[7,18,1,128]{3,2,1,0:T(1,128)S(1)} %get-tuple-element.67), channel_id=1, source_target_pairs={{1,0},{2,1},{3,2},{5,4},{6,5},{7,6},{9,8},{10,9},{11,10},{13,12},{... | collective-permute-start | bytes 193544 | tf_op jit(solution)/shard_map/ppermute | solution.py:23
  87.7 4.8 %collective-permute-start.13 = (f32[7,1,32,128]{3,2,1,0:T(8,128)S(1)}, f32[7,1,32,128]{3,2,1,0:T(8,128)S(1)}, u32[]{:S(2)}, u32[]{:S(2)}) collective-permute-start(f32[7,1,32,128]{3,2,1,0:T(8,128)S(1)} %get-tuple-element.72), channel_id=1, source_target_pairs={{0,4},{4,8},{8,12},{12,16},{16,20},{20,24},{24,28},{28,32},{32,36}... | collective-permute-start | bytes 344072 | tf_op jit(solution)/shard_map/ppermute | solution.py:20
  90.6 14.2 %collective-permute-start.12 = (f32[7,1,32,128]{3,2,1,0:T(8,128)S(1)}, f32[7,1,32,128]{3,2,1,0:T(8,128)S(1)}, u32[]{:S(2)}, u32[]{:S(2)}) collective-permute-start(f32[7,1,32,128]{3,2,1,0:T(8,128)S(1)} %get-tuple-element.73), channel_id=1, source_target_pairs={{4,0},{8,4},{12,8},{16,12},{20,16},{24,20},{28,24},{32,28},{36,32}... | collective-permute-start | bytes 344072 | tf_op jit(solution)/shard_map/ppermute | solution.py:23
  104.9 4.3 %collective-permute-start.15 = (f32[7,18,1,128]{3,2,1,0:T(1,128)S(1)}, f32[7,18,1,128]{3,2,1,0:T(1,128)S(1)}, u32[]{:S(2)}, u32[]{:S(2)}) collective-permute-start(f32[7,18,1,128]{3,2,1,0:T(1,128)S(1)} %get-tuple-element.64), channel_id=1, source_target_pairs={{0,1},{1,2},{2,3},{4,5},{5,6},{6,7},{8,9},{9,10},{10,11},{12,13},{... | collective-permute-start | bytes 193544 | tf_op jit(solution)/shard_map/ppermute | solution.py:20
  107.9 5.0 %collective-permute-start.14 = (f32[7,18,1,128]{3,2,1,0:T(1,128)S(1)}, f32[7,18,1,128]{3,2,1,0:T(1,128)S(1)}, u32[]{:S(2)}, u32[]{:S(2)}) collective-permute-start(f32[7,18,1,128]{3,2,1,0:T(1,128)S(1)} %get-tuple-element.65), channel_id=1, source_target_pairs={{1,0},{2,1},{3,2},{5,4},{6,5},{7,6},{9,8},{10,9},{11,10},{13,12},{... | collective-permute-start | bytes 193544 | tf_op jit(solution)/shard_map/ppermute | solution.py:23
  119.6 5.4 %collective-permute-start.17 = (f32[7,1,32,128]{3,2,1,0:T(8,128)S(1)}, f32[7,1,32,128]{3,2,1,0:T(8,128)S(1)}, u32[]{:S(2)}, u32[]{:S(2)}) collective-permute-start(f32[7,1,32,128]{3,2,1,0:T(8,128)S(1)} %get-tuple-element.70), channel_id=1, source_target_pairs={{0,4},{4,8},{8,12},{12,16},{16,20},{20,24},{24,28},{28,32},{32,36}... | collective-permute-start | bytes 344072 | tf_op jit(solution)/shard_map/ppermute | solution.py:20
  122.8 14.2 %collective-permute-start.16 = (f32[7,1,32,128]{3,2,1,0:T(8,128)S(1)}, f32[7,1,32,128]{3,2,1,0:T(8,128)S(1)}, u32[]{:S(2)}, u32[]{:S(2)}) collective-permute-start(f32[7,1,32,128]{3,2,1,0:T(8,128)S(1)} %get-tuple-element.71), channel_id=1, source_target_pairs={{4,0},{8,4},{12,8},{16,12},{20,16},{24,20},{28,24},{32,28},{36,32}... | collective-permute-start | bytes 344072 | tf_op jit(solution)/shard_map/ppermute | solution.py:23
  137.2 3.0 %collective-permute-start.19 = (f32[7,18,1,128]{3,2,1,0:T(1,128)S(1)}, f32[7,18,1,128]{3,2,1,0:T(1,128)S(1)}, u32[]{:S(2)}, u32[]{:S(2)}) collective-permute-start(f32[7,18,1,128]{3,2,1,0:T(1,128)S(1)} %get-tuple-element.62), channel_id=1, source_target_pairs={{0,1},{1,2},{2,3},{4,5},{5,6},{6,7},{8,9},{9,10},{10,11},{12,13},{... | collective-permute-start | bytes 193544 | tf_op jit(solution)/shard_map/ppermute | solution.py:20
  138.8 5.0 %collective-permute-start.18 = (f32[7,18,1,128]{3,2,1,0:T(1,128)S(1)}, f32[7,18,1,128]{3,2,1,0:T(1,128)S(1)}, u32[]{:S(2)}, u32[]{:S(2)}) collective-permute-start(f32[7,18,1,128]{3,2,1,0:T(1,128)S(1)} %get-tuple-element.63), channel_id=1, source_target_pairs={{1,0},{2,1},{3,2},{5,4},{6,5},{7,6},{9,8},{10,9},{11,10},{13,12},{... | collective-permute-start | bytes 193544 | tf_op jit(solution)/shard_map/ppermute | solution.py:23
  150.4 1.2 copy-start.3
where the time goes:
time: 153 us
  waiting for transfers between devices  60.8 us (40%)
  starting transfers between devices  60.2 us (39%)
  other arithmetic  26.7 us (17%)
  local copies, waits for them, and re-layouts  4.37 us (3%)
    ppermute x10, waiting for transfers between devices, extended(): lax.ppermute(lax.slice_in_dim(block, 0, width, axis=dim), axis, backward)  60.8 us
    ppermute x10, starting transfers between devices, extended(): lax.ppermute(lax.slice_in_dim(block, block.shape[dim] - width, None, axis...  44 us
    concatenate x7, other arithmetic, extended(): block = jnp.concatenate([low, block, high], axis=dim)  16.4 us
    ppermute x10, starting transfers between devices, extended(): lax.ppermute(lax.slice_in_dim(block, 0, width, axis=dim), axis, backward)  16.2 us
    unnamed x24, other arithmetic  6.77 us
  transfers between devices with their start and end apart: 20, of which 8 were waited for; matrix products, arithmetic and copies ran while one was open for 2% of the time, Pallas kernels for 0%

commit v1 on v0

v1 whole, which is shorter than its diff:
```python
import jax
import jax.numpy as jnp
from jax import lax
from jax.experimental import pallas as pl
from jax.experimental.pallas import tpu as pltpu
from jax.sharding import PartitionSpec as P

BLOCK = 16
ITERS = 4
HALO = ITERS
FIELDS = 11
PARTS = 9
F32 = jnp.float32
MIB = 1 << 20

VM = pl.BlockSpec(memory_space=pltpu.VMEM)
HBM = pl.BlockSpec(memory_space=pl.ANY)
SM = pl.BlockSpec(memory_space=pltpu.SMEM)


def params(mib):
    return pltpu.CompilerParams(vmem_limit_bytes=mib * MIB)


def lane_blocks(active, row, shape):
    lane = lax.broadcasted_iota(jnp.int32, shape, 1) // BLOCK
    out = jnp.zeros(shape, jnp.int32)
    for k in range(active.shape[2]):
        out = jnp.where(lane == k, active[0, row, k], out)
    return out


def rolled(v, step, axis):
    n = v.shape[axis]
    return pltpu.roll(v, (n - step) % n, axis)


def shift_z(v, step, fill):
    lane = lax.broadcasted_iota(jnp.int32, v.shape, 1)
    edge = v.shape[1] - 1 if step > 0 else 0
    return jnp.where(lane == edge, fill, rolled(v, step, 1))


def collide(h, hu, a, bc):
    s = 0.25 * h[0] + 0.125 * ((h[1] + h[2]) + (h[3] + h[4]) + (h[5] + h[6]))
    s = s + hu[0] * (h[1] - h[2]) + hu[1] * (h[3] - h[4]) + hu[2] * (h[5] - h[6])
    t = a * s
    return [t + bc * one for one in h]


def pulled_yz(g, nyp, nym, nzp, nzm):
    return [
        rolled(g[3], 1, 0) + nyp * g[4],
        rolled(g[4], -1, 0) + nym * g[3],
        shift_z(g[5], 1, 0.0) + nzp * g[6],
        shift_z(g[6], -1, 0.0) + nzm * g[5],
    ]


def solid_flags(a):
    nf = jnp.where(a > 0.0, 0.0, 1.0).astype(F32)
    return nf, rolled(nf, 1, 0), rolled(nf, -1, 0), shift_z(nf, 1, 1.0), shift_z(nf, -1, 1.0), (1.0 - nf) - a


def pack_y(even, active, g, vel, omega, solid, msg_c, msg_d, gb, vb, ob, sb, sem):
    is_even = even[0] == 1
    ny = omega.shape[1]
    copies = []
    for side in range(2):
        row = (ny - 8) * side
        for n, (src, dst) in enumerate(((g, gb), (vel, vb), (omega, ob), (solid, sb))):
            window = src.at[:, :, pl.ds(row, 8), :] if len(src.shape) == 4 else src.at[:, pl.ds(row, 8), :]
            copies.append(pltpu.make_async_copy(window, dst.at[side], sem.at[side, n]))
    for copy in copies:
        copy.start()
    acts = [lane_blocks(active, (active.shape[1] - 1) * side, (8, 128)) for side in range(2)]
    for copy in copies:
        copy.wait()

    def plane(x, _):
        out = []
        for side in range(2):
            rows = slice(4, 8) if side else slice(0, 4)
            f = ((1 - sb[side, x]) * acts[side]).astype(F32)
            vals = [gb[side, c, x] * f for c in range(7)] + [0.5 * vb[side, c, x] for c in range(3)] + [f * ob[side, x]]
            out.append([v[rows] for v in vals])
        for c in range(FIELDS):
            low, high = out[0][c], out[1][c]
            msg_c[c, x] = jnp.where(is_even, high, low)
            msg_d[c, x] = jnp.where(is_even, low, high)
        return 0

    lax.fori_loop(0, omega.shape[0], plane, 0)


def gather_plane(x, is_even, acts, gb, vb, ob, sb, rc, rd, put):
    ny = ob.shape[1]
    half = ny // len(acts)
    f = jnp.concatenate([((1 - sb[x, n * half:(n + 1) * half]) * act).astype(F32) for n, act in enumerate(acts)], axis=0)
    for c in range(FIELDS):
        own = gb[c, x] * f if c < 7 else 0.5 * vb[c - 7, x] if c < 10 else f * ob[x]
        one, two = rc[c, x], rd[c, x]
        put(c, slice(0, HALO), jnp.where(is_even, two, one))
        put(c, slice(HALO, HALO + ny), own)
        put(c, slice(HALO + ny, 2 * HALO + ny), jnp.where(is_even, one, two))


def all_acts(active, ny):
    nb = active.shape[1]
    return [lane_blocks(active, n, (ny // nb, 128)) for n in range(nb)]


def faces(even, active, g, vel, omega, solid, rc, rd, msg_a, msg_b, st, gb, vb, ob, sb, work, sem):
    y_even, is_even = even[0] == 1, even[1] == 1
    nx, ny = omega.shape[0], omega.shape[1]
    copies = []
    for side in range(2):
        first = (nx - 4) * side
        for n, (src, dst) in enumerate(((g, gb), (vel, vb), (omega, ob), (solid, sb))):
            window = src.at[:, pl.ds(first, 4)] if len(src.shape) == 4 else src.at[pl.ds(first, 4)]
            into = dst.at[:, pl.ds(4 * side, 4)] if len(src.shape) == 4 else dst.at[pl.ds(4 * side, 4)]
            copies.append(pltpu.make_async_copy(window, into, sem.at[side, n]))
    for copy in copies:
        copy.start()
    acts = all_acts(active, ny)
    for copy in copies:
        copy.wait()

    for which in range(2):
        msg = (msg_a, msg_b)[which]
        right = is_even if which == 0 else jnp.logical_not(is_even)
        sign = jnp.where(right, 1.0, -1.0).astype(F32)
        for p in range(4):
            local = jnp.where(right, 7 - p, p)
            halo = jnp.where(right, nx - 1 - p, p)
            half = ny // len(acts)
            f = jnp.concatenate([((1 - sb[local, n * half:(n + 1) * half]) * act).astype(F32) for n, act in enumerate(acts)], axis=0)
            for c in range(FIELDS):
                real = c if c not in (1, 2) else jnp.where(right, c, 3 - c)
                own = gb[real, local] * f if c < 7 else 0.5 * vb[c - 7, local] if c < 10 else f * ob[local]
                one, two = rc[real, halo], rd[real, halo]
                low, high = jnp.where(y_even, two, one), jnp.where(y_even, one, two)
                if c == 7:
                    own, low, high = own * sign, low * sign, high * sign
                to = work.at[0, c, p] if c < 7 else st.at[which, c - 7, p]
                to[0:HALO] = low
                to[HALO:HALO + ny] = own
                to[HALO + ny:2 * HALO + ny] = high
        msg[0] = work[0, 2, 0]
        for c in range(4):
            plane = st[which, c, 0]
            msg[4 + c] = plane * sign if c == 0 else plane
        msg[8] = st[which, 3, 1] * (0.125 + st[which, 0, 1])
        flags = [solid_flags(st[which, 3, p]) for p in range(4)]
        for t in range(1, 4):
            old, new = (t - 1) % 2, t % 2
            for p in range(4 - t):
                gs = [work[old, c, p] for c in range(7)]
                nf, nyp, nym, nzp, nzm, bc = flags[p]
                if p == 0:
                    h1 = jnp.zeros_like(gs[0])
                else:
                    h1 = work[old, 1, p - 1] + flags[p - 1][0] * gs[2]
                h2 = work[old, 2, p + 1] + flags[p + 1][0] * gs[1]
                h = [gs[0], h1, h2] + pulled_yz(gs, nyp, nym, nzp, nzm)
                out = collide(h, [st[which, c, p] for c in range(3)], st[which, 3, p], bc)
                if t == 3:
                    msg[t] = out[2]
                else:
                    for c in range(7):
                        work[new, c, p] = out[c]
                    if p == 0:
                        msg[t] = out[2]


def interior(even, active, g, vel, omega, solid, rc, rd, out, ping, pong, stat, nfs):
    is_even = even[0] == 1
    nx, ny = omega.shape[0], omega.shape[1]
    acts = all_acts(active, ny)
    for buf in (ping, pong):
        for c in (1, 2):
            for x in (0, nx + 1):
                buf[c, x] = jnp.zeros(buf.shape[2:], F32)
    for x in (0, nx + 1):
        nfs[x] = jnp.zeros(nfs.shape[1:], F32)

    def build(x, _):
        def put(c, rows, value):
            if c < 7:
                ping[c, x + 1, rows] = value
            else:
                stat[c - 7, x, rows] = value

        gather_plane(x, is_even, acts, g, vel, omega, solid, rc, rd, put)
        nf, nyp, nym, nzp, nzm, bc = solid_flags(stat[3, x])
        nfs[x + 1] = nf
        for n, v in enumerate((bc, nyp, nym, nzp, nzm)):
            stat[4 + n, x] = v
        return 0

    lax.fori_loop(0, nx, build, 0)
    for t in range(ITERS):
        old, new = (ping, pong) if t % 2 == 0 else (pong, ping)

        def plane(x, _):
            gs = [old[c, x + 1] for c in range(7)]
            h1 = old[1, x + 2] + nfs[x + 2] * gs[2]
            h2 = old[2, x] + nfs[x] * gs[1]
            h = [gs[0], h1, h2] + pulled_yz(gs, stat[5, x], stat[6, x], stat[7, x], stat[8, x])
            res = collide(h, [stat[c, x] for c in range(3)], stat[3, x], stat[4, x])
            for c in range(7):
                if t == ITERS - 1:
                    out[c, x] = res[c][HALO:HALO + ny]
                else:
                    new[c, x + 1] = res[c]
            return 0

        lax.fori_loop(0, nx, plane, 0)


def respond(even, msg_a, msg_b, rec_a, rec_b, st, base, out, near, work, sem):
    is_even = even[0] == 1
    nx, ny = base.shape[1], base.shape[2]
    loads = [pltpu.make_async_copy(base.at[:, pl.ds((nx - 4) * s, 4)], near.at[:, pl.ds(4 * s, 4)], sem.at[s]) for s in range(2)]
    stores = [pltpu.make_async_copy(near.at[:, pl.ds(4 * s, 4)], out.at[:, pl.ds((nx - 4) * s, 4)], sem.at[s]) for s in range(2)]
    for copy in loads:
        copy.start()
    for copy in loads:
        copy.wait()
    for which in range(2):
        mine, theirs = ((msg_a, rec_a), (msg_b, rec_b))[which]
        right = is_even if which == 0 else jnp.logical_not(is_even)
        sign = jnp.where(right, 1.0, -1.0).astype(F32)
        hu = {1: [theirs[4] * sign, theirs[5], theirs[6]]}
        a = {1: theirs[7]}
        for p in range(4):
            hu[2 + p] = [st[which, c, p] for c in range(3)]
            a[2 + p] = st[which, 3, p]
        flags = {q: solid_flags(a[q]) for q in range(1, 6)}
        nf = {q: flags[q][0] for q in range(1, 6)}
        nf[0] = jnp.where(theirs[8] > 0.0, 0.0, 1.0).astype(F32)
        live = set()
        for t in range(ITERS):
            old, new = t % 2, (t + 1) % 2
            source = {2: theirs[t] + nf[1] * mine[t], 1: mine[t] + nf[2] * theirs[t]}

            def comp(q, c):
                return work[old, c, q] if q in live else None

            todo = ((1, 2), (0, 1, 2, 3), (1, 2, 3, 4), (2, 3, 4, 5))[t]
            for q in todo:
                if q == 0:
                    work[new, 1, 0] = theirs[8] * work[old, 2, 1]
                    continue
                gs = [comp(q, c) for c in range(7)]
                zero = jnp.zeros_like(a[q])
                here = q in live
                if here:
                    h = [gs[0], nf[q - 1] * gs[2], nf[q + 1] * gs[1] if q < 5 else zero] + pulled_yz(gs, *flags[q][1:5])
                else:
                    h = [zero] * 7
                if q - 1 in live:
                    h[1] = h[1] + work[old, 1, q - 1]
                if q + 1 in live and q >= 1:
                    h[2] = h[2] + work[old, 2, q + 1]
                if q == 2:
                    h[1] = h[1] + source[2]
                if q == 1:
                    h[2] = h[2] + source[1]
                res = collide(h, hu[q], a[q], flags[q][5])
                if t == ITERS - 1:
                    p = q - 2
                    local = jnp.where(right, 7 - p, p)
                    for c in range(7):
                        real = c if c not in (1, 2) else jnp.where(right, c, 3 - c)
                        near[real, local] = near[real, local] + res[c][HALO:HALO + ny]
                else:
                    for c in range(7):
                        work[new, c, q] = res[c]
            live = set(todo)
    for copy in stores:
        copy.start()
    for copy in stores:
        copy.wait()


def pair_up(x, axis, first):
    pairs = []
    for i in range(first, lax.axis_size(axis) - 1, 2):
        pairs += [(i, i + 1), (i + 1, i)]
    return lax.ppermute(x, axis, pairs)


def call(kernel, outs, ins, out_specs, scratch, mib, cost, **more):
    return pl.pallas_call(
        kernel,
        out_shape=outs,
        in_specs=ins,
        out_specs=out_specs,
        scratch_shapes=scratch,
        compiler_params=params(mib),
        cost_estimate=pl.CostEstimate(flops=cost, bytes_accessed=8 * MIB, transcendentals=0),
        **more,
    )


def on_device(sensitivity, velocity, omega, solid, active):
    nx, ny, nz = omega.shape
    rows = ny + 2 * HALO
    f32 = lambda *shape: jax.ShapeDtypeStruct(shape, F32)
    even_x = (1 - lax.axis_index("gx") % 2).astype(jnp.int32)[None]
    even_y = (1 - lax.axis_index("gy") % 2).astype(jnp.int32)[None]
    vm = pltpu.VMEM
    dma = pltpu.SemaphoreType.DMA

    msg_c, msg_d = call(
        pack_y,
        (f32(FIELDS, nx, HALO, nz),) * 2,
        [SM, SM, HBM, HBM, HBM, HBM],
        (VM, VM),
        [vm((2, 7, nx, 8, nz), F32), vm((2, 3, nx, 8, nz), F32), vm((2, nx, 8, nz), F32), vm((2, nx, 8, nz), jnp.int32), dma((2, 4))],
        24,
        1 << 20,
    )(even_y, active, sensitivity, velocity, omega, solid)
    rec_c = pair_up(msg_c, "gy", 0)
    rec_d = pair_up(msg_d, "gy", 1)

    even = jnp.concatenate([even_y, even_x])
    msg_a, msg_b, st = call(
        faces,
        (f32(PARTS, rows, nz),) * 2 + (f32(2, 4, 4, rows, nz),),
        [SM, SM, HBM, HBM, HBM, HBM, VM, VM],
        (VM, VM, VM),
        [vm((7, 8, ny, nz), F32), vm((3, 8, ny, nz), F32), vm((8, ny, nz), F32), vm((8, ny, nz), jnp.int32), vm((2, 7, 4, rows, nz), F32), dma((2, 4))],
        24,
        1 << 20,
    )(even, active, sensitivity, velocity, omega, solid, rec_c, rec_d)
    rec_a = pair_up(msg_a, "gx", 0)
    rec_b = pair_up(msg_b, "gx", 1)

    base = call(
        interior,
        f32(7, nx, ny, nz),
        [SM, SM, VM, VM, VM, VM, VM, VM],
        VM,
        [vm((7, nx + 2, rows, nz), F32), vm((7, nx + 2, rows, nz), F32), vm((9, nx, rows, nz), F32), vm((nx + 2, rows, nz), F32)],
        32,
        1 << 24,
    )(even_y, active, sensitivity, velocity, omega, solid, rec_c, rec_d)

    return call(
        respond,
        f32(7, nx, ny, nz),
        [SM, VM, VM, VM, VM, VM, HBM],
        HBM,
        [vm((7, 8, ny, nz), F32), vm((2, 7, 6, rows, nz), F32), dma((2,))],
        24,
        1 << 20,
        input_output_aliases={6: 0},
    )(even_x, msg_a, msg_b, rec_a, rec_b, st, base)


def solution(mesh):
    in_specs = (
        P(None, "gx", "gy", None),
        P(None, "gx", "gy", None),
        P("gx", "gy", None),
        P("gx", "gy", None),
        P("gx", "gy", None),
    )
    out_specs = P(None, "gx", "gy", None)
    return jax.shard_map(
        on_device, mesh=mesh, in_specs=in_specs, out_specs=out_specs, check_vma=False
    )
```

time: 153 us -> 49.7 us (0.32)
  the two profiles are of different devices: /device:TPU:231 before, /device:TPU:456 now
where the time goes in v1:
time: 49.7 us; the launch traced here: 49.3 us
  starting transfers between devices  17.9 us (36%)
  Pallas kernels  17.6 us (35%)
  waiting for transfers between devices  8.35 us (17%)
  local copies, waits for them, and re-layouts  5.24 us (11%)
    ppermute x4, starting transfers between devices, pair_up(): return lax.ppermute(x, axis, pairs)  17.9 us
    pallas_call x1, Pallas kernels, on_device(): call(interior, f32(7, nx, ny, nz), [SM, SM, VM, VM, VM, VM, VM, VM], VM,...  10.1 us
    ppermute x4, waiting for transfers between devices, pair_up(): return lax.ppermute(x, axis, pairs)  8.35 us
    unnamed x20, local copies, waits for them, and re-layouts  5.24 us
    pallas_call x1, Pallas kernels, on_device(): call(respond, f32(7, nx, ny, nz), [SM, VM, VM, VM, VM, VM, HBM], HBM, [vm...  3.01 us
    pallas_call x1, Pallas kernels, on_device(): call(faces, (f32(PARTS, rows, nz),) * 2 + (f32(2, 4, 4, rows, nz),), [SM,...  2.42 us
    pallas_call x1, Pallas kernels, on_device(): call(pack_y, (f32(FIELDS, nx, HALO, nz),) * 2, [SM, SM, HBM, HBM, HBM, HB...  2.02 us
  transfers between devices with their start and end apart: 4, of which 2 were waited for; matrix products, arithmetic and copies ran while one was open for 0% of the time, Pallas kernels for 21%

profile of v1, /device:TPU:456, one launch (start us, length us, event | category | flops | bytes accessed | tf_op | source)
XLA Modules:
  0.0 49.3 jit_solution(12879086979211841145)
XLA Ops:
  0.0 0.0 copy-start.9
  0.0 1.5 %copy-done = f32[7,16,32,128]{3,2,1,0:T(8,128)S(1)} copy-done((f32[7,16,32,128]{3,2,1,0:T(8,128)S(1)}, f32[7,16,32,128]{3,2,1,0:T(8,128)}, u32[]{:S(2)}) %copy-start) | copy-done | bytes 1835032
  1.5 1.1 %copy-done.2 = f32[3,16,32,128]{3,2,1,0:T(8,128)S(1)} copy-done((f32[3,16,32,128]{3,2,1,0:T(8,128)S(1)}, f32[3,16,32,128]{3,2,1,0:T(8,128)}, u32[]{:S(2)}) %copy-start.2) | copy-done | bytes 786456
  2.7 0.9 %copy-done.4 = f32[16,32,128]{2,1,0:T(8,128)S(1)} copy-done((f32[16,32,128]{2,1,0:T(8,128)S(1)}, f32[16,32,128]{2,1,0:T(8,128)}, u32[]{:S(2)}) %copy-start.4) | copy-done | bytes 262168
  3.6 0.9 %copy-done.6 = s32[16,32,128]{2,1,0:T(8,128)S(1)} copy-done((s32[16,32,128]{2,1,0:T(8,128)S(1)}, s32[16,32,128]{2,1,0:T(8,128)}, u32[]{:S(2)}) %copy-start.6) | copy-done | bytes 262168
  4.6 0.7 %copy-done.8 = s32[1,2,8]{2,1,0:T(2,128)S(1)} copy-done((s32[1,2,8]{2,1,0:T(2,128)S(1)}, s32[1,2,8]{2,1,0:T(2,128)}, u32[]{:S(2)}) %copy-start.8) | copy-done | bytes 88
  5.2 2.0 %shard_map.55 = (f32[11,16,4,128]{3,2,1,0:T(4,128)}, f32[11,16,4,128]{3,2,1,0:T(4,128)}) custom-call(s32[1]{0:T(128)} %bitcast.1.even, s32[1,2,8]{2,1,0:T(2,128)S(1)} %copy-done.8, f32[7,16,32,128]{3,2,1,0:T(8,128)S(1)} %copy-done, f32[3,16,32,128]{3,2,1,0:T(8,128)S(1)} %copy-done.2, f32[16,32,128]{2,1,0:T(8,128)S(1)} %copy-done.4, s32[16,32,128]{2,1,0:T(8,128)S(1)} %copy-done.6), custom_call_target="tpu_custom_call" | custom-call | flops 1048576 | bytes 8388608 | tf_op jit(solution)/shard_map/pallas_call | solution.py:316
  7.3 2.4 %collective-permute-start = (f32[11,16,4,128]{3,2,1,0:T(4,128)}, f32[11,16,4,128]{3,2,1,0:T(4,128)S(1)}, u32[]{:S(2)}, u32[]{:S(2)}) collective-permute-start(f32[11,16,4,128]{3,2,1,0:T(4,128)} %get-tuple-element.10), channel_id=1, source_target_pairs={{0,1},{1,0},{2,3},{3,2},{4,5},{5,4},{6,7},{7,6},{8,9},{9,8},{10,11... | collective-permute-start | bytes 1081352 | tf_op jit(solution)/shard_map/ppermute | solution.py:291
  9.6 4.6 %collective-permute-start.1 = (f32[11,16,4,128]{3,2,1,0:T(4,128)}, f32[11,16,4,128]{3,2,1,0:T(4,128)}, u32[]{:S(2)}, u32[]{:S(2)}) collective-permute-start(f32[11,16,4,128]{3,2,1,0:T(4,128)} %get-tuple-element.11), channel_id=1, source_target_pairs={{1,2},{2,1},{5,6},{6,5},{9,10},{10,9},{13,14},{14,13},{17,18},{18,... | collective-permute-start | bytes 1081352 | tf_op jit(solution)/shard_map/ppermute | solution.py:291
  14.3 0.1 pad_add_fusion.even
  14.3 5.2 %collective-permute-done.rc = f32[11,16,4,128]{3,2,1,0:T(4,128)S(1)} collective-permute-done((f32[11,16,4,128]{3,2,1,0:T(4,128)}, f32[11,16,4,128]{3,2,1,0:T(4,128)S(1)}, u32[]{:S(2)}, u32[]{:S(2)}) %collective-permute-start) | collective-permute-done | bytes 360480 | tf_op jit(solution)/shard_map/ppermute | solution.py:291
  19.5 3.2 %collective-permute-done.1.rd = f32[11,16,4,128]{3,2,1,0:T(4,128)} collective-permute-done((f32[11,16,4,128]{3,2,1,0:T(4,128)}, f32[11,16,4,128]{3,2,1,0:T(4,128)}, u32[]{:S(2)}, u32[]{:S(2)}) %collective-permute-start.1) | collective-permute-done | bytes 360480 | tf_op jit(solution)/shard_map/ppermute | solution.py:291
  22.7 0.0 copy-done.9
  22.7 0.0 copy-done.1
  22.7 0.0 copy-done.3
  22.7 0.0 copy-done.5
  22.7 0.0 copy-done.7
  22.7 2.4 %shard_map.56 = (f32[9,40,128]{2,1,0:T(8,128)S(1)}, f32[9,40,128]{2,1,0:T(8,128)S(1)}, f32[2,4,4,40,128]{4,3,2,1,0:T(8,128)S(1)}) custom-call(s32[2]{0:T(128)S(1)} %pad_add_fusion.even, s32[1,2,8]{2,1,0:T(2,128)S(1)} %copy-done.9, f32[7,16,32,128]{3,2,1,0:T(8,128)S(1)} %copy-done.1, f32[3,16,32,128]{3,2,1,0:T(8,128)S(1)} %copy-done.3, ...), custom_call_target="tpu_custom_call" | custom-call | flops 1048576 | bytes 8388608 | tf_op jit(solution)/shard_map/pallas_call | solution.py:329
  25.1 1.9 %collective-permute-start.2 = (f32[9,40,128]{2,1,0:T(8,128)S(1)}, f32[9,40,128]{2,1,0:T(8,128)S(1)}, u32[]{:S(2)}, u32[]{:S(2)}) collective-permute-start(f32[9,40,128]{2,1,0:T(8,128)S(1)} %get-tuple-element.12.msg_a), channel_id=1, source_target_pairs={{0,4},{4,0},{8,12},{12,8},{16,20},{20,16},{24,28},{28,24},{32,36},... | collective-permute-start | bytes 552968 | tf_op jit(solution)/shard_map/ppermute | solution.py:291
  27.1 9.1 %collective-permute-start.3 = (f32[9,40,128]{2,1,0:T(8,128)S(1)}, f32[9,40,128]{2,1,0:T(8,128)S(1)}, u32[]{:S(2)}, u32[]{:S(2)}) collective-permute-start(f32[9,40,128]{2,1,0:T(8,128)S(1)} %get-tuple-element.13.msg_b), channel_id=1, source_target_pairs={{4,8},{8,4},{12,16},{16,12},{20,24},{24,20},{28,32},{32,28},{36,40... | collective-permute-start | bytes 552968 | tf_op jit(solution)/shard_map/ppermute | solution.py:291
  36.1 10.1 %shard_map.57.base = f32[7,16,32,128]{3,2,1,0:T(8,128)} custom-call(s32[1]{0:T(128)} %bitcast.1.even, s32[1,2,8]{2,1,0:T(2,128)S(1)} %copy-done.9, f32[7,16,32,128]{3,2,1,0:T(8,128)S(1)} %copy-done.1, f32[3,16,32,128]{3,2,1,0:T(8,128)S(1)} %copy-done.3, f32[16,32,128]{2,1,0:T(8,128)S(1)} %copy-done.5, s32[16,32,128]{2,1,0:T(8,128)S(1)} %copy-done.7, ...), custom_call_target="tpu_custom_call" | custom-call | flops 16777216 | bytes 8388608 | tf_op jit(solution)/shard_map/pallas_call | solution.py:341
  46.3 0.0 collective-permute-done.2.rec_a
  46.3 0.0 collective-permute-done.3.rec_b
  46.3 3.0 %shard_map.58 = f32[7,16,32,128]{3,2,1,0:T(8,128)} custom-call(s32[1]{0:T(128)} %bitcast.even, f32[9,40,128]{2,1,0:T(8,128)S(1)} %get-tuple-element.12.msg_a, f32[9,40,128]{2,1,0:T(8,128)S(1)} %get-tuple-element.13.msg_b, f32[9,40,128]{2,1,0:T(8,128)S(1)} %collective-permute-done.2.rec_a, ...), custom_call_target="tpu_custom_call", output_to_operand_aliasing={{}: (6, {})} | custom-call | flops 1048576 | bytes 8388608 | tf_op jit(solution)/shard_map/pallas_call | solution.py:351
  (9 shorter events, 0.0 us)
Async XLA Ops:
  0.0 22.7 %copy-start.9 = (s32[1,2,8]{2,1,0:T(2,128)S(1)}, s32[1,2,8]{2,1,0:T(2,128)}, u32[]{:S(2)}) copy-start(s32[1,2,8]{2,1,0:T(2,128)} %active.5) | copy-start | bytes 196
  0.0 1.5 %copy-start = (f32[7,16,32,128]{3,2,1,0:T(8,128)S(1)}, f32[7,16,32,128]{3,2,1,0:T(8,128)}, u32[]{:S(2)}) copy-start(f32[7,16,32,128]{3,2,1,0:T(8,128)} %g.5) | copy-start | bytes 5505028
  1.5 1.1 %copy-start.2 = (f32[3,16,32,128]{3,2,1,0:T(8,128)S(1)}, f32[3,16,32,128]{3,2,1,0:T(8,128)}, u32[]{:S(2)}) copy-start(f32[3,16,32,128]{3,2,1,0:T(8,128)} %vel.5) | copy-start | bytes 2359300
  2.6 0.9 %copy-start.4 = (f32[16,32,128]{2,1,0:T(8,128)S(1)}, f32[16,32,128]{2,1,0:T(8,128)}, u32[]{:S(2)}) copy-start(f32[16,32,128]{2,1,0:T(8,128)} %omega.5) | copy-start | bytes 786436
  3.6 0.9 %copy-start.6 = (s32[16,32,128]{2,1,0:T(8,128)S(1)}, s32[16,32,128]{2,1,0:T(8,128)}, u32[]{:S(2)}) copy-start(s32[16,32,128]{2,1,0:T(8,128)} %solid.5) | copy-start | bytes 786436
  4.6 0.7 %copy-start.8 = (s32[1,2,8]{2,1,0:T(2,128)S(1)}, s32[1,2,8]{2,1,0:T(2,128)}, u32[]{:S(2)}) copy-start(s32[1,2,8]{2,1,0:T(2,128)} %active.5) | copy-start | bytes 196
  5.2 17.5 %copy-start.1 = (f32[7,16,32,128]{3,2,1,0:T(8,128)S(1)}, f32[7,16,32,128]{3,2,1,0:T(8,128)}, u32[]{:S(2)}) copy-start(f32[7,16,32,128]{3,2,1,0:T(8,128)} %g.5) | copy-start | bytes 5505028
  5.2 17.5 %copy-start.3 = (f32[3,16,32,128]{3,2,1,0:T(8,128)S(1)}, f32[3,16,32,128]{3,2,1,0:T(8,128)}, u32[]{:S(2)}) copy-start(f32[3,16,32,128]{3,2,1,0:T(8,128)} %vel.5) | copy-start | bytes 2359300
  5.2 17.5 %copy-start.5 = (f32[16,32,128]{2,1,0:T(8,128)S(1)}, f32[16,32,128]{2,1,0:T(8,128)}, u32[]{:S(2)}) copy-start(f32[16,32,128]{2,1,0:T(8,128)} %omega.5) | copy-start | bytes 786436
  5.2 17.5 %copy-start.7 = (s32[16,32,128]{2,1,0:T(8,128)S(1)}, s32[16,32,128]{2,1,0:T(8,128)}, u32[]{:S(2)}) copy-start(s32[16,32,128]{2,1,0:T(8,128)} %solid.5) | copy-start | bytes 786436
  7.3 12.3 %collective-permute-start = (f32[11,16,4,128]{3,2,1,0:T(4,128)}, f32[11,16,4,128]{3,2,1,0:T(4,128)S(1)}, u32[]{:S(2)}, u32[]{:S(2)}) collective-permute-start(f32[11,16,4,128]{3,2,1,0:T(4,128)} %get-tuple-element.10), channel_id=1, source_target_pairs={{0,1},{1,0},{2,3},{3,2},{4,5},{5,4},{6,7},{7,6},{8,9},{9,8},{10,11... | collective-permute-start | bytes 1081352 | tf_op jit(solution)/shard_map/ppermute | solution.py:291
  9.6 13.1 %collective-permute-start.1 = (f32[11,16,4,128]{3,2,1,0:T(4,128)}, f32[11,16,4,128]{3,2,1,0:T(4,128)}, u32[]{:S(2)}, u32[]{:S(2)}) collective-permute-start(f32[11,16,4,128]{3,2,1,0:T(4,128)} %get-tuple-element.11), channel_id=1, source_target_pairs={{1,2},{2,1},{5,6},{6,5},{9,10},{10,9},{13,14},{14,13},{17,18},{18,... | collective-permute-start | bytes 1081352 | tf_op jit(solution)/shard_map/ppermute | solution.py:291
  25.1 21.1 %collective-permute-start.2 = (f32[9,40,128]{2,1,0:T(8,128)S(1)}, f32[9,40,128]{2,1,0:T(8,128)S(1)}, u32[]{:S(2)}, u32[]{:S(2)}) collective-permute-start(f32[9,40,128]{2,1,0:T(8,128)S(1)} %get-tuple-element.12.msg_a), channel_id=1, source_target_pairs={{0,4},{4,0},{8,12},{12,8},{16,20},{20,16},{24,28},{28,24},{32,36},... | collective-permute-start | bytes 552968 | tf_op jit(solution)/shard_map/ppermute | solution.py:291
  27.1 19.2 %collective-permute-start.3 = (f32[9,40,128]{2,1,0:T(8,128)S(1)}, f32[9,40,128]{2,1,0:T(8,128)S(1)}, u32[]{:S(2)}, u32[]{:S(2)}) collective-permute-start(f32[9,40,128]{2,1,0:T(8,128)S(1)} %get-tuple-element.13.msg_b), channel_id=1, source_target_pairs={{4,8},{8,4},{12,16},{16,12},{20,24},{24,20},{28,32},{32,28},{36,40... | collective-permute-start | bytes 552968 | tf_op jit(solution)/shard_map/ppermute | solution.py:291

commit v2 on v0

v2 whole, which is shorter than its diff:
```python
import functools

import jax
import jax.numpy as jnp
from jax import lax
from jax.experimental import pallas as pl
from jax.experimental.pallas import tpu as pltpu
from jax.sharding import PartitionSpec as P

BLOCK = 16
ITERS = 4
TILE = 8
FIELDS = 11
FLUX = FIELDS
CORNER = FIELDS + 4
ROWS = CORNER + 2
PARTS = 9
F32 = jnp.float32
MIB = 1 << 20

VM = pl.BlockSpec(memory_space=pltpu.VMEM)
HBM = pl.BlockSpec(memory_space=pl.ANY)
SM = pl.BlockSpec(memory_space=pltpu.SMEM)


def params(mib):
    return pltpu.CompilerParams(vmem_limit_bytes=mib * MIB)


def even_index(axis):
    return lax.axis_index(axis) % 2 == 0


def lane_blocks(active, row, shape):
    lane = lax.broadcasted_iota(jnp.int32, shape, 1) // BLOCK
    out = jnp.zeros(shape, jnp.int32)
    for k in range(active.shape[2]):
        out = jnp.where(lane == k, active[0, row, k], out)
    return out


def rolled(v, step, axis):
    n = v.shape[axis]
    return pltpu.roll(v, (n - step) % n, axis)


def shift_z(v, step, fill):
    lane = lax.broadcasted_iota(jnp.int32, v.shape, 1)
    edge = v.shape[1] - 1 if step > 0 else 0
    return jnp.where(lane == edge, fill, rolled(v, step, 1))


def collide(h, hu, a, bc):
    s = 0.25 * h[0] + 0.125 * ((h[1] + h[2]) + (h[3] + h[4]) + (h[5] + h[6]))
    s = s + hu[0] * (h[1] - h[2]) + hu[1] * (h[3] - h[4]) + hu[2] * (h[5] - h[6])
    t = a * s
    return [t + bc * one for one in h]


def write_flags(a_ref, flags):
    a = a_ref[...]
    nf = jnp.where(a > 0.0, 0.0, 1.0).astype(F32)
    flags[0] = rolled(nf, 1, 0)
    flags[1] = rolled(nf, -1, 0)
    flags[2] = shift_z(nf, 1, 1.0)
    flags[3] = shift_z(nf, -1, 1.0)
    flags[4] = (1.0 - nf) - a
    flags[5] = nf


def advance(tiles, g, pull_1, pull_2, hu, a, flags, put, drop=None):
    if g is not None:
        g3, g4 = g[3][...], g[4][...]
        up, down = rolled(g3, 1, 0), rolled(g4, -1, 0)
    for i in range(tiles):
        r = slice(TILE * i, TILE * i + TILE)
        if g is None:
            zero = jnp.zeros((TILE, a.shape[1]), F32)
            h = [zero, pull_1(r, zero), pull_2(r, zero), zero, zero, zero, zero]
        else:
            g1, g2, g5, g6 = (g[c][r] for c in (1, 2, 5, 6))
            h = [
                g[0][r],
                pull_1(r, g2),
                pull_2(r, g1),
                up[r] + flags[0, r] * g4[r],
                down[r] + flags[1, r] * g3[r],
                shift_z(g5, 1, 0.0) + flags[2, r] * g6,
                shift_z(g6, -1, 0.0) + flags[3, r] * g5,
            ]
        if drop is not None:
            h[drop] = jnp.zeros_like(h[drop])
        put(r, collide(h, [one[r] for one in hu], a[r], flags[4, r]), h)


def pack_rows(active, g, vel, omega, solid, msg_c, msg_d, gb, vb, ob, sb, ping, pong, stat, fl, sem):
    is_even = even_index("gy")
    nx, ny = omega.shape[0], omega.shape[1]
    copies = []
    for side in range(2):
        row = (ny - TILE) * side
        for n, (src, dst) in enumerate(((solid, sb), (omega, ob), (vel, vb), (g, gb))):
            window = src.at[:, :, pl.ds(row, TILE), :] if len(src.shape) == 4 else src.at[:, pl.ds(row, TILE), :]
            copies.append(pltpu.make_async_copy(window, dst.at[side], sem.at[side, n]))
    for copy in copies:
        copy.start()
    acts = [lane_blocks(active, (active.shape[1] - 1) * side, (TILE, 128)) for side in range(2)]
    zero = jnp.zeros((TILE, 128), F32)
    for side in range(2):
        for x in (0, nx + 1):
            fl[side, x, 5] = zero
            for c in (1, 2):
                ping[side, c, x] = zero
                pong[side, c, x] = zero
    for copy in copies:
        copy.wait()

    def send(k, x, values, row):
        low, high = values[0][row:row + 1], values[1][TILE - 1 - row:TILE - row]
        msg_c[k, x] = jnp.where(is_even, high, low)
        msg_d[k, x] = jnp.where(is_even, low, high)

    def build(x, _):
        fields = []
        for side in range(2):
            f = ((1 - sb[side, x]) * acts[side]).astype(F32)
            vals = [gb[side, c, x] * f for c in range(7)] + [0.5 * vb[side, c, x] for c in range(3)] + [f * ob[side, x]]
            for c in range(FIELDS):
                if c < 7:
                    ping[side, c, x + 1] = vals[c]
                else:
                    stat[side, c - 7, x] = vals[c]
            write_flags(stat.at[side, 3, x], fl.at[side, x + 1])
            fields.append(vals)
        for c in range(FIELDS):
            send(c, x, [fields[0][c], fields[1][c]], 0)
        send(FLUX, x, [fields[0][3], fields[1][4]], 1)
        send(FLUX + 3, x, [fields[0][10] * (0.125 - fields[0][8]), fields[1][10] * (0.125 + fields[1][8])], 1)
        return 0

    lax.fori_loop(0, nx, build, 0, unroll=16)

    def step(x, t):
        old, new = (ping, pong) if t == 0 else (pong, ping)
        fluxes = []
        for side in range(2):

            def pull_1(r, g2):
                return old[side, 1, x + 2, r] + fl[side, x + 2, 5, r] * g2

            def pull_2(r, g1):
                return old[side, 2, x, r] + fl[side, x, 5, r] * g1

            def put(r, res, h):
                if t == 0:
                    for c in range(7):
                        new[side, c, x + 1, r] = res[c]
                fluxes.append(res[3 + side])

            gs = [old.at[side, c, x + 1] for c in range(7)]
            advance(1, gs, pull_1, pull_2, [stat.at[side, c, x] for c in range(3)], stat.at[side, 3, x], fl.at[side, x + 1], put, None if t == 0 else 4 - side)
        send(FLUX + 1 + t, x, fluxes, 1)

    for t in range(2):

        def plane(x, _):
            step(x, t)
            return 0

        lax.fori_loop(0, nx, plane, 0, unroll=16)

    for face in range(2):
        at = [nx - 1 if face else 0, nx - 2 if face else 1]
        for n, (p, row) in enumerate(((0, 1), (0, 2), (1, 1))):
            for c in range(4):
                send(CORNER + face, 4 * n + c, [stat[side, c, at[p]] for side in range(2)], row)
        for n, (buf, row) in enumerate(((None, 1), (pong, 1), (None, 2))):
            if buf is None:
                f = [((1 - sb[side, at[0]]) * acts[side]).astype(F32) for side in range(2)]
                send(CORNER + face, 12 + n, [gb[side, 1 + face, at[0]] * f[side] for side in range(2)], row)
            else:
                send(CORNER + face, 12 + n, [buf[side, 1 + face, at[0] + 1] for side in range(2)], row)
        msg_c[CORNER + face, 15] = zero[:1]
        msg_d[CORNER + face, 15] = zero[:1]


def halo_rows(rc, rd, y_even):
    def row(k, x):
        one, two = rc[k, x], rd[k, x]
        return jnp.where(y_even, one, two), jnp.where(y_even, two, one)

    return row


def placed(tile, rows, at):
    sub = lax.broadcasted_iota(jnp.int32, (TILE, 128), 0)
    return jnp.where(sub == at, rows[0], jnp.where(sub == TILE - 1 - at, rows[1], tile))


def with_flux(res, h, rows, t, x):
    sub = lax.broadcasted_iota(jnp.int32, (TILE, 128), 0)
    high, low = rows(FLUX + t, x)
    if t == 2:
        k = rows(FLUX + 3, x)
        high, low = high + k[0] * h[4], low + k[1] * h[3]
    res[3] = jnp.where(sub == 1, high, res[3])
    res[4] = jnp.where(sub == TILE - 2, low, res[4])


def all_acts(active, ny):
    nb = active.shape[1]
    return [lane_blocks(active, n, (ny // nb, 128)) for n in range(nb)]


def gather_plane(x, acts, g, vel, omega, solid, halo, dest, mirror):
    ny = omega.shape[1]
    half = ny // len(acts)
    f = jnp.concatenate([((1 - solid[x, n * half:(n + 1) * half]) * act).astype(F32) for n, act in enumerate(acts)], axis=0)
    for c in range(FIELDS):
        real = c
        if mirror is not None and c in (1, 2):
            real = jnp.where(mirror[0], c, 3 - c)
        own = g[real, x] * f if c < 7 else 0.5 * vel[c - 7, x] if c < 10 else f * omega[x]
        rest = halo(real)
        if mirror is not None and c == 7:
            own, rest = own * mirror[1], rest * mirror[1]
        to = dest(c)
        to[0:ny] = own
        to[ny:ny + TILE] = rest


def face(which, active, g, vel, omega, solid, rc, rd, msg, st, work, fl):
    y_even, x_even = even_index("gy"), even_index("gx")
    nx, ny = omega.shape[0], omega.shape[1]
    tiles = work.shape[3] // TILE
    right = x_even if which == 0 else jnp.logical_not(x_even)
    sign = jnp.where(right, 1.0, -1.0).astype(F32)
    acts = all_acts(active, ny)
    rows = halo_rows(rc, rd, y_even)
    corner = jnp.where(right, CORNER + 1, CORNER)
    where = [jnp.where(right, nx - 1 - p, p) for p in range(4)]
    for p in range(4):

        def halo(c):
            tile = placed(jnp.zeros((TILE, 128), F32), rows(c, where[p]), 0)
            if isinstance(c, int) and c in (3, 4):
                high, low = rows(FLUX, where[p])
                sub = lax.broadcasted_iota(jnp.int32, (TILE, 128), 0)
                tile = jnp.where(sub == (1 if c == 3 else TILE - 2), high if c == 3 else low, tile)
            if isinstance(c, int) and c >= 7:
                if p == 0:
                    tile = placed(placed(tile, rows(corner, c - 7), 1), rows(corner, c - 3), 2)
                if p == 1:
                    tile = placed(tile, rows(corner, c + 1), 1)
            return tile

        gather_plane(where[p], acts, g, vel, omega, solid, halo, lambda c: work.at[0, c, p] if c < 7 else st.at[c - 7, p], (right, sign))
        write_flags(st.at[3, p], fl.at[p])
    last = slice(ny, ny + TILE)
    msg[0, 0:ny] = work[0, 2, 0, 0:ny]
    msg[0, last] = placed(placed(work[0, 2, 0, last], rows(corner, 12), 1), rows(corner, 14), 2)
    msg[4] = st[0, 0] * sign
    for c in range(1, 4):
        msg[4 + c] = st[c, 0]
    msg[8] = st[3, 1] * (0.125 + st[0, 1])
    for t in range(1, 4):
        old, new = (t - 1) % 2, t % 2
        for p in range(4 - t):

            def pull_1(r, g2):
                if p == 0:
                    return jnp.zeros_like(g2)
                return work[old, 1, p - 1, r] + fl[p - 1, 5, r] * g2

            def pull_2(r, g1):
                return work[old, 2, p + 1, r] + fl[p + 1, 5, r] * g1

            def put(r, out, h):
                if t == 1 and r == last:
                    with_flux(out, h, rows, t, where[p])
                if p == 0:
                    msg[t, r] = placed(out[2], rows(corner, 13), 1) if t == 1 and r == last else out[2]
                if t < 3:
                    for c in range(7):
                        work[new, c, p, r] = out[c]

            gs = [work.at[old, c, p] for c in range(7)]
            advance(tiles, gs, pull_1, pull_2, [st.at[c, p] for c in range(3)], st.at[3, p], fl.at[p], put)


def interior(active, g, vel, omega, solid, rc, rd, out, near, ping, pong, stat, fl, mid, sem):
    y_even = even_index("gy")
    nx, ny = omega.shape[0], omega.shape[1]
    tiles = ping.shape[2] // TILE
    acts = all_acts(active, ny)
    rows = halo_rows(rc, rd, y_even)
    for x in (0, nx + 1):
        for buf in (ping, pong):
            for c in (1, 2):
                buf[c, x] = jnp.zeros(buf.shape[2:], F32)
        fl[x, 5] = jnp.zeros(fl.shape[2:], F32)

    def build(x, _):
        def halo(c):
            tile = placed(jnp.zeros((TILE, 128), F32), rows(c, x), 0)
            sub = lax.broadcasted_iota(jnp.int32, (TILE, 128), 0)
            if c in (3, 4):
                high, low = rows(FLUX, x)
                tile = jnp.where(sub == (1 if c == 3 else TILE - 2), high if c == 3 else low, tile)
            if c == 10:
                tile = placed(tile, rows(FLUX + 3, x), 1)
            return tile

        gather_plane(x, acts, g, vel, omega, solid, halo, lambda c: ping.at[c, x + 1] if c < 7 else stat.at[c - 7, x], None)
        write_flags(stat.at[3, x], fl.at[x + 1])
        return 0

    lax.fori_loop(0, nx, build, 0, unroll=16)

    for t in range(ITERS):
        old, new = (ping, pong) if t % 2 == 0 else (pong, ping)

        def run(x, tiles, put):
            def pull_1(r, g2):
                return old[1, x + 2, r] + fl[x + 2, 5, r] * g2

            def pull_2(r, g1):
                return old[2, x, r] + fl[x, 5, r] * g1

            gs = [old.at[c, x + 1] for c in range(7)]
            advance(tiles, gs, pull_1, pull_2, [stat.at[c, x] for c in range(3)], stat.at[3, x], fl.at[x + 1], put)

        if t < ITERS - 1:

            def plane(x, _):
                def put(r, res, h):
                    if t < 2 and r.start == ny:
                        with_flux(res, h, rows, t + 1, x)
                    for c in range(7):
                        new[c, x + 1, r] = res[c]

                run(x, tiles, put)
                return 0

            lax.fori_loop(0, nx, plane, 0, unroll=16)
        else:

            def last(into, shift):
                def plane(x, _):
                    def put(r, res, h):
                        for c in range(7):
                            into[c, x - shift, r] = res[c]

                    run(x, ny // TILE, put)
                    return 0

                return plane

            lax.fori_loop(4, nx - 4, last(mid, 4), 0, unroll=4)
            store = pltpu.make_async_copy(mid, out.at[:, pl.ds(4, nx - 8)], sem.at[0])
            store.start()
            lax.fori_loop(0, 4, last(near, 0), 0, unroll=4)
            lax.fori_loop(nx - 4, nx, last(near, nx - 8), 0, unroll=4)
            store.wait()


def respond(msg_a, msg_b, rec_a, rec_b, st_a, st_b, near, base, out, work, fl, hu1, done, sem):
    is_even = even_index("gx")
    nx, ny = base.shape[1], base.shape[2]
    tiles = work.shape[3] // TILE
    for which in range(2):
        mine, theirs, st = ((msg_a, rec_a, st_a), (msg_b, rec_b, st_b))[which]
        right = is_even if which == 0 else jnp.logical_not(is_even)
        sign = jnp.where(right, 1.0, -1.0).astype(F32)
        hu1[...] = theirs[4] * sign
        hu = {1: [hu1, theirs.at[5], theirs.at[6]]}
        a = {1: theirs.at[7]}
        for p in range(4):
            hu[2 + p] = [st.at[c, p] for c in range(3)]
            a[2 + p] = st.at[3, p]
        for q in range(1, 6):
            write_flags(a[q], fl.at[q])
        fl[0, 5] = jnp.where(theirs[8] > 0.0, 0.0, 1.0).astype(F32)
        live = set()
        for t in range(ITERS):
            old, new = t % 2, (t + 1) % 2
            todo = ((1, 2), (0, 1, 2, 3), (1, 2, 3, 4), (2, 3, 4, 5))[t]
            for q in todo:
                if q == 0:
                    work[new, 1, 0] = theirs[8] * work[old, 2, 1]
                    continue

                def pull_1(r, g2):
                    h = fl[q - 1, 5, r] * g2 if q in live else g2
                    if q - 1 in live:
                        h = h + work[old, 1, q - 1, r]
                    if q == 2:
                        h = h + (theirs[t, r] + fl[1, 5, r] * mine[t, r])
                    return h

                def pull_2(r, g1):
                    h = fl[q + 1, 5, r] * g1 if q in live else g1
                    if q + 1 in live:
                        h = h + work[old, 2, q + 1, r]
                    if q == 1:
                        h = h + (mine[t, r] + fl[2, 5, r] * theirs[t, r])
                    return h

                def put(r, res, h):
                    if t < ITERS - 1:
                        for c in range(7):
                            work[new, c, q, r] = res[c]
                        return
                    local = jnp.where(right, 9 - q, q - 2)
                    for c in range(7):
                        real = c if c not in (1, 2) else jnp.where(right, c, 3 - c)
                        done[real, local, r] = near[real, local, r] + res[c]

                gs = [work.at[old, c, q] for c in range(7)] if q in live else None
                advance(tiles if t < ITERS - 1 else ny // TILE, gs, pull_1, pull_2, hu[q], a[q], fl.at[q], put)
            live = set(todo)
        if which == 0:
            first = jnp.where(right, 1, 0)
            store = pltpu.make_async_copy(done.at[:, pl.ds(4 * first, 4)], out.at[:, pl.ds((nx - 4) * first, 4)], sem.at[0])
            store.start()
    first = 1 - first
    other = pltpu.make_async_copy(done.at[:, pl.ds(4 * first, 4)], out.at[:, pl.ds((nx - 4) * first, 4)], sem.at[1])
    other.start()
    store.wait()
    other.wait()


def pair_up(x, axis, first):
    pairs = []
    for i in range(first, lax.axis_size(axis) - 1, 2):
        pairs += [(i, i + 1), (i + 1, i)]
    return lax.ppermute(x, axis, pairs)


def call(kernel, outs, ins, out_specs, scratch, mib, cost, **more):
    return pl.pallas_call(
        kernel,
        out_shape=outs,
        in_specs=ins,
        out_specs=out_specs,
        scratch_shapes=scratch,
        compiler_params=params(mib),
        cost_estimate=pl.CostEstimate(flops=cost, bytes_accessed=4 * MIB, transcendentals=0),
        **more,
    )


def on_device(sensitivity, velocity, omega, solid, active):
    nx, ny, nz = omega.shape
    rows = ny + TILE
    f32 = lambda *shape: jax.ShapeDtypeStruct(shape, F32)
    vm = pltpu.VMEM
    dma = pltpu.SemaphoreType.DMA

    pinned = [pltpu.with_memory_space_constraint(v, pltpu.HBM) for v in (active, sensitivity, velocity, omega, solid)]
    edge = lambda *shape: vm((2,) + shape + (TILE, nz), F32)
    msg_c, msg_d = call(
        pack_rows,
        (f32(ROWS, nx, 1, nz),) * 2,
        [SM, HBM, HBM, HBM, HBM],
        (VM,) * 2,
        [edge(7, nx), edge(3, nx), edge(nx), vm((2, nx, TILE, nz), jnp.int32), edge(7, nx + 2), edge(7, nx + 2), edge(4, nx), edge(nx + 2, 6), dma((2, 4))],
        24,
        1 << 20,
    )(*pinned)
    rec_c = pair_up(msg_c, "gy", 0)
    rec_d = pair_up(msg_d, "gy", 1)

    def message(which):
        return call(
            functools.partial(face, which),
            (f32(PARTS, rows, nz), f32(4, 4, rows, nz)),
            [SM, VM, VM, VM, VM, VM, VM],
            (VM, VM),
            [vm((2, 7, 4, rows, nz), F32), vm((4, 6, rows, nz), F32)],
            24,
            1 << 20,
        )(active, sensitivity, velocity, omega, solid, rec_c, rec_d)

    msg_b, st_b = message(1)
    rec_b = pair_up(msg_b, "gx", 1)
    msg_a, st_a = message(0)
    rec_a = pair_up(msg_a, "gx", 0)

    base, near = call(
        interior,
        (f32(7, nx, ny, nz), f32(7, 8, ny, nz)),
        [SM, VM, VM, VM, VM, VM, VM],
        (HBM, VM),
        [
            vm((7, nx + 2, rows, nz), F32),
            vm((7, nx + 2, rows, nz), F32),
            vm((4, nx, rows, nz), F32),
            vm((nx + 2, 6, rows, nz), F32),
            vm((7, nx - 8, ny, nz), F32),
            dma((1,)),
        ],
        32,
        1 << 24,
    )(active, sensitivity, velocity, omega, solid, rec_c, rec_d)

    return call(
        respond,
        f32(7, nx, ny, nz),
        [VM, VM, VM, VM, VM, VM, VM, HBM],
        HBM,
        [vm((2, 7, 6, rows, nz), F32), vm((6, 6, rows, nz), F32), vm((rows, nz), F32), vm((7, 8, ny, nz), F32), dma((2,))],
        24,
        1 << 20,
        input_output_aliases={7: 0},
    )(msg_a, msg_b, rec_a, rec_b, st_a, st_b, near, base)


def solution(mesh):
    in_specs = (
        P(None, "gx", "gy", None),
        P(None, "gx", "gy", None),
        P("gx", "gy", None),
        P("gx", "gy", None),
        P("gx", "gy", None),
    )
    out_specs = P(None, "gx", "gy", None)
    return jax.shard_map(
        on_device, mesh=mesh, in_specs=in_specs, out_specs=out_specs, check_vma=False
    )
```

time: 153 us -> 32.1 us (0.21)
  the two profiles are of different devices: /device:TPU:231 before, /device:TPU:264 now
where the time goes in v2:
time: 32.1 us; the launch traced here: 31.9 us
  starting transfers between devices  15.2 us (47%)
  Pallas kernels  10.5 us (33%)
  waiting for transfers between devices  6.06 us (19%)
    ppermute x4, starting transfers between devices, pair_up(): return lax.ppermute(x, axis, pairs)  15.2 us
    ppermute x4, waiting for transfers between devices, pair_up(): return lax.ppermute(x, axis, pairs)  6.06 us
    pallas_call x1, Pallas kernels, on_device(): call(interior, (f32(7, nx, ny, nz), f32(7, 8, ny, nz)), [SM, VM, VM, VM,...  4.12 us
    pallas_call x1, Pallas kernels, on_device(): call(pack_rows, (f32(ROWS, nx, 1, nz),) * 2, [SM, HBM, HBM, HBM, HBM], (V...  3.06 us
    pallas_call x2, Pallas kernels, message(): call(functools.partial(face, which), (f32(PARTS, rows, nz), f32(4, 4, row...  1.79 us
    pallas_call x1, Pallas kernels, on_device(): call(respond, f32(7, nx, ny, nz), [VM, VM, VM, VM, VM, VM, VM, HBM], HBM,...  1.57 us
  transfers between devices with their start and end apart: 4, of which 3 were waited for; matrix products, arithmetic and copies ran while one was open for 0% of the time, Pallas kernels for 16%

profile of v2, /device:TPU:264, one launch (start us, length us, event | category | flops | bytes accessed | tf_op | source)
XLA Modules:
  0.0 31.9 jit_solution(2850632701561530218)
XLA Ops:
  0.0 0.0 copy-start.4
  0.0 0.0 copy-start.3
  0.0 0.0 copy-start.2
  0.0 0.0 copy-start.1
  0.0 0.0 copy-start
  0.0 3.1 %shard_map.55 = (f32[17,16,1,128]{3,2,1,0:T(1,128)S(1)}, f32[17,16,1,128]{3,2,1,0:T(1,128)S(1)}) custom-call(s32[1,2,8]{2,1,0:T(2,128)} %active.7, f32[7,16,32,128]{3,2,1,0:T(8,128)} %g.7, f32[3,16,32,128]{3,2,1,0:T(8,128)} %vel.7, f32[16,32,128]{2,1,0:T(8,128)} %omega.7, s32[16,32,128]{2,1,0:T(8,128)} %solid.7), custom_call_target="tpu_custom_call" | custom-call | flops 1048576 | bytes 4194304 | tf_op jit(solution)/shard_map/pallas_call | solution.py:462
  3.1 2.4 %collective-permute-start = (f32[17,16,1,128]{3,2,1,0:T(1,128)S(1)}, f32[17,16,1,128]{3,2,1,0:T(1,128)S(1)}, u32[]{:S(2)}, u32[]{:S(2)}) collective-permute-start(f32[17,16,1,128]{3,2,1,0:T(1,128)S(1)} %get-tuple-element.13), channel_id=1, source_target_pairs={{0,1},{1,0},{2,3},{3,2},{4,5},{5,4},{6,7},{7,6},{8,9},{9,8},{10,11... | collective-permute-start | bytes 417800 | tf_op jit(solution)/shard_map/ppermute | solution.py:437
  5.5 4.6 %collective-permute-start.1 = (f32[17,16,1,128]{3,2,1,0:T(1,128)S(1)}, f32[17,16,1,128]{3,2,1,0:T(1,128)S(1)}, u32[]{:S(2)}, u32[]{:S(2)}) collective-permute-start(f32[17,16,1,128]{3,2,1,0:T(1,128)S(1)} %get-tuple-element.14), channel_id=1, source_target_pairs={{1,2},{2,1},{5,6},{6,5},{9,10},{10,9},{13,14},{14,13},{17,18},{18,... | collective-permute-start | bytes 417800 | tf_op jit(solution)/shard_map/ppermute | solution.py:437
  10.1 0.3 %collective-permute-done.rc = f32[17,16,1,128]{3,2,1,0:T(1,128)S(1)} collective-permute-done((f32[17,16,1,128]{3,2,1,0:T(1,128)S(1)}, f32[17,16,1,128]{3,2,1,0:T(1,128)S(1)}, u32[]{:S(2)}, u32[]{:S(2)}) %collective-permute-start) | collective-permute-done | bytes 139296 | tf_op jit(solution)/shard_map/ppermute | solution.py:437
  10.4 3.1 %collective-permute-done.1.rd = f32[17,16,1,128]{3,2,1,0:T(1,128)S(1)} collective-permute-done((f32[17,16,1,128]{3,2,1,0:T(1,128)S(1)}, f32[17,16,1,128]{3,2,1,0:T(1,128)S(1)}, u32[]{:S(2)}, u32[]{:S(2)}) %collective-permute-start.1) | collective-permute-done | bytes 139296 | tf_op jit(solution)/shard_map/ppermute | solution.py:437
  13.5 0.0 copy-done.4
  13.5 0.0 copy-done.3
  13.5 0.0 copy-done.2
  13.5 0.0 copy-done.1
  13.5 0.0 copy-done
  13.5 0.9 %shard_map.57 = (f32[9,40,128]{2,1,0:T(8,128)S(1)}, f32[4,4,40,128]{3,2,1,0:T(8,128)S(1)}) custom-call(s32[1,2,8]{2,1,0:T(2,128)S(1)} %copy-done.4, f32[7,16,32,128]{3,2,1,0:T(8,128)S(1)} %copy-done, f32[3,16,32,128]{3,2,1,0:T(8,128)S(1)} %copy-done.1, f32[16,32,128]{2,1,0:T(8,128)S(1)} %copy-done.2, s32[16,32,128]{2,1,0:T(8,128)S(1)} %copy-done.3, ...), custom_call_target="tpu_custom_call" | custom-call | flops 1048576 | bytes 4194304 | tf_op jit(solution)/shard_map/pallas_call | solution.py:475
  14.4 6.3 %collective-permute-start.3 = (f32[9,40,128]{2,1,0:T(8,128)S(1)}, f32[9,40,128]{2,1,0:T(8,128)S(1)}, u32[]{:S(2)}, u32[]{:S(2)}) collective-permute-start(f32[9,40,128]{2,1,0:T(8,128)S(1)} %get-tuple-element.16.msg_b), channel_id=1, source_target_pairs={{4,8},{8,4},{12,16},{16,12},{20,24},{24,20},{28,32},{32,28},{36,40... | collective-permute-start | bytes 552968 | tf_op jit(solution)/shard_map/ppermute | solution.py:437
  20.7 0.9 %shard_map.56 = (f32[9,40,128]{2,1,0:T(8,128)S(1)}, f32[4,4,40,128]{3,2,1,0:T(8,128)S(1)}) custom-call(s32[1,2,8]{2,1,0:T(2,128)S(1)} %copy-done.4, f32[7,16,32,128]{3,2,1,0:T(8,128)S(1)} %copy-done, f32[3,16,32,128]{3,2,1,0:T(8,128)S(1)} %copy-done.1, f32[16,32,128]{2,1,0:T(8,128)S(1)} %copy-done.2, s32[16,32,128]{2,1,0:T(8,128)S(1)} %copy-done.3, ...), custom_call_target="tpu_custom_call" | custom-call | flops 1048576 | bytes 4194304 | tf_op jit(solution)/shard_map/pallas_call | solution.py:475
  21.6 1.9 %collective-permute-start.2 = (f32[9,40,128]{2,1,0:T(8,128)S(1)}, f32[9,40,128]{2,1,0:T(8,128)S(1)}, u32[]{:S(2)}, u32[]{:S(2)}) collective-permute-start(f32[9,40,128]{2,1,0:T(8,128)S(1)} %get-tuple-element.15.msg_a), channel_id=1, source_target_pairs={{0,4},{4,0},{8,12},{12,8},{16,20},{20,16},{24,28},{28,24},{32,36},... | collective-permute-start | bytes 552968 | tf_op jit(solution)/shard_map/ppermute | solution.py:437
  23.5 4.1 %shard_map.58 = (f32[7,16,32,128]{3,2,1,0:T(8,128)}, f32[7,8,32,128]{3,2,1,0:T(8,128)S(1)}) custom-call(s32[1,2,8]{2,1,0:T(2,128)S(1)} %copy-done.4, f32[7,16,32,128]{3,2,1,0:T(8,128)S(1)} %copy-done, f32[3,16,32,128]{3,2,1,0:T(8,128)S(1)} %copy-done.1, f32[16,32,128]{2,1,0:T(8,128)S(1)} %copy-done.2, s32[16,32,128]{2,1,0:T(8,128)S(1)} %copy-done.3, ...), custom_call_target="tpu_custom_call" | custom-call | flops 16777216 | bytes 4194304 | tf_op jit(solution)/shard_map/pallas_call | solution.py:490
  27.6 2.7 %collective-permute-done.3.rec_b = f32[9,40,128]{2,1,0:T(8,128)S(1)} collective-permute-done((f32[9,40,128]{2,1,0:T(8,128)S(1)}, f32[9,40,128]{2,1,0:T(8,128)S(1)}, u32[]{:S(2)}, u32[]{:S(2)}) %collective-permute-start.3) | collective-permute-done | bytes 184352 | tf_op jit(solution)/shard_map/ppermute | solution.py:437
  30.3 0.0 collective-permute-done.2.rec_a
  30.3 1.6 %shard_map.59 = f32[7,16,32,128]{3,2,1,0:T(8,128)} custom-call(f32[9,40,128]{2,1,0:T(8,128)S(1)} %get-tuple-element.15.msg_a, f32[9,40,128]{2,1,0:T(8,128)S(1)} %get-tuple-element.16.msg_b, f32[9,40,128]{2,1,0:T(8,128)S(1)} %collective-permute-done.2.rec_a, f32[9,40,128]{2,1,0:T(8,128)S(1)} %collective-permute-done.3.rec_b, ...), custom_call_target="tpu_custom_call", output_to_operand_aliasing={{}: (7, {})} | custom-call | flops 1048576 | bytes 4194304 | tf_op jit(solution)/shard_map/pallas_call | solution.py:507
Async XLA Ops:
  0.0 13.5 %copy-start.4 = (s32[1,2,8]{2,1,0:T(2,128)S(1)}, s32[1,2,8]{2,1,0:T(2,128)}, u32[]{:S(2)}) copy-start(s32[1,2,8]{2,1,0:T(2,128)} %active.7) | copy-start | bytes 196
  0.0 13.5 %copy-start.3 = (s32[16,32,128]{2,1,0:T(8,128)S(1)}, s32[16,32,128]{2,1,0:T(8,128)}, u32[]{:S(2)}) copy-start(s32[16,32,128]{2,1,0:T(8,128)} %solid.7) | copy-start | bytes 786436
  0.0 13.5 %copy-start.2 = (f32[16,32,128]{2,1,0:T(8,128)S(1)}, f32[16,32,128]{2,1,0:T(8,128)}, u32[]{:S(2)}) copy-start(f32[16,32,128]{2,1,0:T(8,128)} %omega.7) | copy-start | bytes 786436
  0.0 13.5 %copy-start.1 = (f32[3,16,32,128]{3,2,1,0:T(8,128)S(1)}, f32[3,16,32,128]{3,2,1,0:T(8,128)}, u32[]{:S(2)}) copy-start(f32[3,16,32,128]{3,2,1,0:T(8,128)} %vel.7) | copy-start | bytes 2359300
  0.0 13.5 %copy-start = (f32[7,16,32,128]{3,2,1,0:T(8,128)S(1)}, f32[7,16,32,128]{3,2,1,0:T(8,128)}, u32[]{:S(2)}) copy-start(f32[7,16,32,128]{3,2,1,0:T(8,128)} %g.7) | copy-start | bytes 5505028
  3.1 7.3 %collective-permute-start = (f32[17,16,1,128]{3,2,1,0:T(1,128)S(1)}, f32[17,16,1,128]{3,2,1,0:T(1,128)S(1)}, u32[]{:S(2)}, u32[]{:S(2)}) collective-permute-start(f32[17,16,1,128]{3,2,1,0:T(1,128)S(1)} %get-tuple-element.13), channel_id=1, source_target_pairs={{0,1},{1,0},{2,3},{3,2},{4,5},{5,4},{6,7},{7,6},{8,9},{9,8},{10,11... | collective-permute-start | bytes 417800 | tf_op jit(solution)/shard_map/ppermute | solution.py:437
  5.5 8.0 %collective-permute-start.1 = (f32[17,16,1,128]{3,2,1,0:T(1,128)S(1)}, f32[17,16,1,128]{3,2,1,0:T(1,128)S(1)}, u32[]{:S(2)}, u32[]{:S(2)}) collective-permute-start(f32[17,16,1,128]{3,2,1,0:T(1,128)S(1)} %get-tuple-element.14), channel_id=1, source_target_pairs={{1,2},{2,1},{5,6},{6,5},{9,10},{10,9},{13,14},{14,13},{17,18},{18,... | collective-permute-start | bytes 417800 | tf_op jit(solution)/shard_map/ppermute | solution.py:437
  14.4 15.9 %collective-permute-start.3 = (f32[9,40,128]{2,1,0:T(8,128)S(1)}, f32[9,40,128]{2,1,0:T(8,128)S(1)}, u32[]{:S(2)}, u32[]{:S(2)}) collective-permute-start(f32[9,40,128]{2,1,0:T(8,128)S(1)} %get-tuple-element.16.msg_b), channel_id=1, source_target_pairs={{4,8},{8,4},{12,16},{16,12},{20,24},{24,20},{28,32},{32,28},{36,40... | collective-permute-start | bytes 552968 | tf_op jit(solution)/shard_map/ppermute | solution.py:437
  21.6 8.7 %collective-permute-start.2 = (f32[9,40,128]{2,1,0:T(8,128)S(1)}, f32[9,40,128]{2,1,0:T(8,128)S(1)}, u32[]{:S(2)}, u32[]{:S(2)}) collective-permute-start(f32[9,40,128]{2,1,0:T(8,128)S(1)} %get-tuple-element.15.msg_a), channel_id=1, source_target_pairs={{0,4},{4,0},{8,12},{12,8},{16,20},{20,16},{24,28},{28,24},{32,36},... | collective-permute-start | bytes 552968 | tf_op jit(solution)/shard_map/ppermute | solution.py:437

commit v3 on v2

--- a/solution.py
+++ b/solution.py
@@ -20,7 +20,6 @@
 
 VM = pl.BlockSpec(memory_space=pltpu.VMEM)
 HBM = pl.BlockSpec(memory_space=pl.ANY)
-SM = pl.BlockSpec(memory_space=pltpu.SMEM)
 
 
 def params(mib):
@@ -34,8 +33,8 @@
 def lane_blocks(active, row, shape):
     lane = lax.broadcasted_iota(jnp.int32, shape, 1) // BLOCK
     out = jnp.zeros(shape, jnp.int32)
-    for k in range(active.shape[2]):
-        out = jnp.where(lane == k, active[0, row, k], out)
+    for k in range(active.shape[1]):
+        out = jnp.where(lane == k, jnp.broadcast_to(active[row:row + 1, k:k + 1], shape), out)
     return out
 
 
@@ -93,7 +92,7 @@
         put(r, collide(h, [one[r] for one in hu], a[r], flags[4, r]), h)
 
 
-def pack_rows(active, g, vel, omega, solid, msg_c, msg_d, gb, vb, ob, sb, ping, pong, stat, fl, sem):
+def pack_rows(active, g, vel, omega, solid, msg_c, msg_d, gb, vb, ob, sb, ab, ping, pong, stat, fl, sem):
     is_even = even_index("gy")
     nx, ny = omega.shape[0], omega.shape[1]
     copies = []
@@ -102,9 +101,9 @@
         for n, (src, dst) in enumerate(((solid, sb), (omega, ob), (vel, vb), (g, gb))):
             window = src.at[:, :, pl.ds(row, TILE), :] if len(src.shape) == 4 else src.at[:, pl.ds(row, TILE), :]
             copies.append(pltpu.make_async_copy(window, dst.at[side], sem.at[side, n]))
-    for copy in copies:
+    copies.append(pltpu.make_async_copy(active, ab, sem.at[2, 0]))
+    for copy in reversed(copies):
         copy.start()
-    acts = [lane_blocks(active, (active.shape[1] - 1) * side, (TILE, 128)) for side in range(2)]
     zero = jnp.zeros((TILE, 128), F32)
     for side in range(2):
         for x in (0, nx + 1):
@@ -112,7 +111,9 @@
             for c in (1, 2):
                 ping[side, c, x] = zero
                 pong[side, c, x] = zero
-    for copy in copies:
+    copies[-1].wait()
+    acts = [lane_blocks(ab[0], (active.shape[1] - 1) * side, (TILE, 128)) for side in range(2)]
+    for copy in copies[:-1]:
         copy.wait()
 
     def send(k, x, values, row):
@@ -209,7 +210,7 @@
 
 def all_acts(active, ny):
     nb = active.shape[1]
-    return [lane_blocks(active, n, (ny // nb, 128)) for n in range(nb)]
+    return [lane_blocks(active[0], n, (ny // nb, 128)) for n in range(nb)]
 
 
 def gather_plane(x, acts, g, vel, omega, solid, halo, dest, mirror):
@@ -229,8 +230,10 @@
         to[ny:ny + TILE] = rest
 
 
-def face(which, active, g, vel, omega, solid, rc, rd, msg, st, work, fl):
+def face(which, active, g, vel, omega, solid, rc, rd, *rest):
+    msg, st, fl, work = rest[-4:]
     y_even, x_even = even_index("gy"), even_index("gx")
+    rc = rc.at[jnp.where(y_even, 1, 0)]
     nx, ny = omega.shape[0], omega.shape[1]
     tiles = work.shape[3] // TILE
     right = x_even if which == 0 else jnp.logical_not(x_even)
@@ -290,6 +293,7 @@
 
 def interior(active, g, vel, omega, solid, rc, rd, out, near, ping, pong, stat, fl, mid, sem):
     y_even = even_index("gy")
+    rc = rc.at[jnp.where(y_even, 1, 0)]
     nx, ny = omega.shape[0], omega.shape[1]
     tiles = ping.shape[2] // TILE
     acts = all_acts(active, ny)
@@ -364,70 +368,68 @@
             store.wait()
 
 
-def respond(msg_a, msg_b, rec_a, rec_b, st_a, st_b, near, base, out, work, fl, hu1, done, sem):
-    is_even = even_index("gx")
-    nx, ny = base.shape[1], base.shape[2]
+def respond(which, mine, got, st, own, near, base, out, work, flags, hu1, done, sem):
+    nx, ny = out.shape[1], out.shape[2]
     tiles = work.shape[3] // TILE
-    for which in range(2):
-        mine, theirs, st = ((msg_a, rec_a, st_a), (msg_b, rec_b, st_b))[which]
-        right = is_even if which == 0 else jnp.logical_not(is_even)
-        sign = jnp.where(right, 1.0, -1.0).astype(F32)
-        hu1[...] = theirs[4] * sign
-        hu = {1: [hu1, theirs.at[5], theirs.at[6]]}
-        a = {1: theirs.at[7]}
-        for p in range(4):
-            hu[2 + p] = [st.at[c, p] for c in range(3)]
-            a[2 + p] = st.at[3, p]
-        for q in range(1, 6):
-            write_flags(a[q], fl.at[q])
-        fl[0, 5] = jnp.where(theirs[8] > 0.0, 0.0, 1.0).astype(F32)
-        live = set()
-        for t in range(ITERS):
-            old, new = t % 2, (t + 1) % 2
-            todo = ((1, 2), (0, 1, 2, 3), (1, 2, 3, 4), (2, 3, 4, 5))[t]
-            for q in todo:
-                if q == 0:
-                    work[new, 1, 0] = theirs[8] * work[old, 2, 1]
-                    continue
-
-                def pull_1(r, g2):
-                    h = fl[q - 1, 5, r] * g2 if q in live else g2
-                    if q - 1 in live:
-                        h = h + work[old, 1, q - 1, r]
-                    if q == 2:
-                        h = h + (theirs[t, r] + fl[1, 5, r] * mine[t, r])
-                    return h
-
-                def pull_2(r, g1):
-                    h = fl[q + 1, 5, r] * g1 if q in live else g1
-                    if q + 1 in live:
-                        h = h + work[old, 2, q + 1, r]
-                    if q == 1:
-                        h = h + (mine[t, r] + fl[2, 5, r] * theirs[t, r])
-                    return h
-
-                def put(r, res, h):
-                    if t < ITERS - 1:
-                        for c in range(7):
-                            work[new, c, q, r] = res[c]
-                        return
-                    local = jnp.where(right, 9 - q, q - 2)
+    right = even_index("gx") if which == 0 else jnp.logical_not(even_index("gx"))
+    sign = jnp.where(right, 1.0, -1.0).astype(F32)
+    theirs = got.at[jnp.where(right, 1, 0)] if which == 0 else got
+    hu1[...] = theirs[4] * sign
+    hu = {1: [hu1, theirs.at[5], theirs.at[6]]}
+    a = {1: theirs.at[7]}
+    fl = {0: flags.at[0], 1: flags.at[1]}
+    for p in range(4):
+        hu[2 + p] = [st.at[c, p] for c in range(3)]
+        a[2 + p] = st.at[3, p]
+        fl[2 + p] = own.at[p]
+    write_flags(a[1], fl[1])
+    fl[0][5] = jnp.where(theirs[8] > 0.0, 0.0, 1.0).astype(F32)
+    live = set()
+    stores = []
+    for t in range(ITERS):
+        old, new = t % 2, (t + 1) % 2
+        todo = ((1, 2), (0, 1, 2, 3), (1, 2, 3, 4), (5, 4, 3, 2))[t]
+        for q in todo:
+            if q == 0:
+                work[new, 1, 0] = theirs[8] * work[old, 2, 1]
+                continue
+
+            def pull_1(r, g2):
+                h = fl[q - 1][5, r] * g2 if q in live else g2
+                if q - 1 in live:
+                    h = h + work[old, 1, q - 1, r]
+                if q == 2:
+                    h = h + (theirs[t, r] + fl[1][5, r] * mine[t, r])
+                return h
+
+            def pull_2(r, g1):
+                h = fl[q + 1][5, r] * g1 if q in live else g1
+                if q + 1 in live:
+                    h = h + work[old, 2, q + 1, r]
+                if q == 1:
+                    h = h + (mine[t, r] + fl[2][5, r] * theirs[t, r])
+                return h
+
+            p = q - 2
+            x = jnp.where(right, 7 - p, p)
+
+            def put(r, res, h):
+                if t < ITERS - 1:
                     for c in range(7):
-                        real = c if c not in (1, 2) else jnp.where(right, c, 3 - c)
-                        done[real, local, r] = near[real, local, r] + res[c]
-
-                gs = [work.at[old, c, q] for c in range(7)] if q in live else None
-                advance(tiles if t < ITERS - 1 else ny // TILE, gs, pull_1, pull_2, hu[q], a[q], fl.at[q], put)
-            live = set(todo)
-        if which == 0:
-            first = jnp.where(right, 1, 0)
-            store = pltpu.make_async_copy(done.at[:, pl.ds(4 * first, 4)], out.at[:, pl.ds((nx - 4) * first, 4)], sem.at[0])
-            store.start()
-    first = 1 - first
-    other = pltpu.make_async_copy(done.at[:, pl.ds(4 * first, 4)], out.at[:, pl.ds((nx - 4) * first, 4)], sem.at[1])
-    other.start()
-    store.wait()
-    other.wait()
+                        work[new, c, q, r] = res[c]
+                    return
+                for c in range(7):
+                    real = c if c not in (1, 2) else jnp.where(right, c, 3 - c)
+                    done[p, real, r] = near[real, x, r] + res[c]
+
+            gs = [work.at[old, c, q] for c in range(7)] if q in live else None
+            advance(tiles if t < ITERS - 1 else ny // TILE, gs, pull_1, pull_2, hu[q], a[q], fl[q], put)
+            if t == ITERS - 1:
+                stores.append(pltpu.make_async_copy(done.at[p], out.at[:, jnp.where(right, nx - 1 - p, p)], sem.at[p]))
+                stores[-1].start()
+        live = set(todo)
+    for store in stores:
+        store.wait()
 
 
 def pair_up(x, axis, first):
@@ -462,35 +464,32 @@
     msg_c, msg_d = call(
         pack_rows,
         (f32(ROWS, nx, 1, nz),) * 2,
-        [SM, HBM, HBM, HBM, HBM],
+        [HBM, HBM, HBM, HBM, HBM],
         (VM,) * 2,
-        [edge(7, nx), edge(3, nx), edge(nx), vm((2, nx, TILE, nz), jnp.int32), edge(7, nx + 2), edge(7, nx + 2), edge(4, nx), edge(nx + 2, 6), dma((2, 4))],
+        [edge(7, nx), edge(3, nx), edge(nx), vm((2, nx, TILE, nz), jnp.int32), vm(active.shape, jnp.int32), edge(7, nx + 2), edge(7, nx + 2), edge(4, nx), edge(nx + 2, 6), dma((3, 4))],
         24,
         1 << 20,
     )(*pinned)
-    rec_c = pair_up(msg_c, "gy", 0)
     rec_d = pair_up(msg_d, "gy", 1)
-
-    def message(which):
+    rec_c = lax.all_gather(msg_c, "gy", axis_index_groups=[[i, i + 1] for i in range(0, lax.axis_size("gy"), 2)])
+
+    def message(which, *after):
         return call(
             functools.partial(face, which),
-            (f32(PARTS, rows, nz), f32(4, 4, rows, nz)),
-            [SM, VM, VM, VM, VM, VM, VM],
-            (VM, VM),
-            [vm((2, 7, 4, rows, nz), F32), vm((4, 6, rows, nz), F32)],
+            (f32(PARTS, rows, nz), f32(4, 4, rows, nz), f32(4, 6, rows, nz)),
+            [VM, VM, VM, VM, VM, VM, VM] + [HBM] * len(after),
+            (VM, VM, VM),
+            [vm((2, 7, 4, rows, nz), F32)],
             24,
             1 << 20,
-        )(active, sensitivity, velocity, omega, solid, rec_c, rec_d)
-
-    msg_b, st_b = message(1)
+        )(active, sensitivity, velocity, omega, solid, rec_c, rec_d, *after)
+
+    msg_b, st_b, fl_b = message(1)
     rec_b = pair_up(msg_b, "gx", 1)
-    msg_a, st_a = message(0)
-    rec_a = pair_up(msg_a, "gx", 0)
-
     base, near = call(
         interior,
         (f32(7, nx, ny, nz), f32(7, 8, ny, nz)),
-        [SM, VM, VM, VM, VM, VM, VM],
+        [VM, VM, VM, VM, VM, VM, VM],
         (HBM, VM),
         [
             vm((7, nx + 2, rows, nz), F32),
@@ -504,16 +503,24 @@
         1 << 24,
     )(active, sensitivity, velocity, omega, solid, rec_c, rec_d)
 
-    return call(
-        respond,
-        f32(7, nx, ny, nz),
-        [VM, VM, VM, VM, VM, VM, VM, HBM],
-        HBM,
-        [vm((2, 7, 6, rows, nz), F32), vm((6, 6, rows, nz), F32), vm((rows, nz), F32), vm((7, 8, ny, nz), F32), dma((2,))],
-        24,
-        1 << 20,
-        input_output_aliases={7: 0},
-    )(msg_a, msg_b, rec_a, rec_b, st_a, st_b, near, base)
+    msg_a, st_a, fl_a = message(0, msg_b)
+    pairs = [[i, i + 1] for i in range(0, lax.axis_size("gx"), 2)]
+    rec_a = lax.all_gather(msg_a, "gx", axis_index_groups=pairs)
+
+    def corrected(which, mine, theirs, st, fl, base):
+        return call(
+            functools.partial(respond, which),
+            f32(7, nx, ny, nz),
+            [VM] * 5 + [HBM],
+            HBM,
+            [vm((2, 7, 6, rows, nz), F32), vm((2, 6, rows, nz), F32), vm((rows, nz), F32), vm((4, 7, ny, nz), F32), dma((4,))],
+            24,
+            1 << 20,
+            input_output_aliases={5: 0},
+        )(mine, theirs, st, fl, near, base)
+
+    base = corrected(0, msg_a, rec_a, st_a, fl_a, base)
+    return corrected(1, msg_b, rec_b, st_b, fl_b, base)
 
 
 def solution(mesh):

time: 32.1 us -> 29.9 us (0.931)
  blocking collectives: 0 us -> 7.88 us
  starting transfers between devices: 15.2 us -> 8.96 us
  waiting for transfers between devices: 6.06 us -> 3.83 us
  Pallas kernels: 10.5 us -> 8.93 us
    all_gather x0 -> x2, blocking collectives: none -> 7.88 us  [the longest x1 5.81 us: on_device(): lax.all_gather(msg_c, 'gy', axis_index_groups=[[i, i + 1] for i in range(...]
    ppermute x4 -> x2, starting transfers between devices: 15.2 us -> 8.96 us  [pair_up(): return lax.ppermute(x, axis, pairs)]
    ppermute x4 -> x2, waiting for transfers between devices: 6.06 us -> 3.83 us  [pair_up(): return lax.ppermute(x, axis, pairs)]
    pallas_call x2, Pallas kernels: 1.79 us -> 0.86 us  [message(): call(functools.partial(face, which), (f32(PARTS, rows, nz), f32(4, 4, row...]
    pallas_call x3 -> x4, Pallas kernels: 8.75 us -> 8.07 us  [the longest x1 3.64 us: on_device(): call(interior, (f32(7, nx, ny, nz), f32(7, 8, ny, nz)), [VM, VM, VM, VM,...]
  transfers between devices with their start and end apart: 4 -> 2, of which waited for: 3 -> 1; matrix products, arithmetic and copies ran while one was open for 0% -> 0% of each run, Pallas kernels for 16% -> 17%
where the time goes in v3:
time: 29.9 us; the launch traced here: 29.7 us
  starting transfers between devices  8.96 us (30%)
  Pallas kernels  8.93 us (30%)
  blocking collectives  7.88 us (26%)
  waiting for transfers between devices  3.83 us (13%)
    ppermute x2, starting transfers between devices, pair_up(): return lax.ppermute(x, axis, pairs)  8.96 us
    all_gather x1, blocking collectives, on_device(): lax.all_gather(msg_c, 'gy', axis_index_groups=[[i, i + 1] for i in range(...  5.81 us
    ppermute x2, waiting for transfers between devices, pair_up(): return lax.ppermute(x, axis, pairs)  3.83 us
    pallas_call x1, Pallas kernels, on_device(): call(interior, (f32(7, nx, ny, nz), f32(7, 8, ny, nz)), [VM, VM, VM, VM,...  3.64 us
    pallas_call x1, Pallas kernels, on_device(): call(pack_rows, (f32(ROWS, nx, 1, nz),) * 2, [HBM, HBM, HBM, HBM, HBM], (...  2.28 us
    pallas_call x2, Pallas kernels, corrected(): call(functools.partial(respond, which), f32(7, nx, ny, nz), [VM] * 5 + [H...  2.15 us
    all_gather x1, blocking collectives, on_device(): rec_a = lax.all_gather(msg_a, 'gx', axis_index_groups=pairs)  2.07 us
    pallas_call x2, Pallas kernels, message(): call(functools.partial(face, which), (f32(PARTS, rows, nz), f32(4, 4, row...  0.86 us
  transfers between devices with their start and end apart: 2, of which 1 were waited for; matrix products, arithmetic and copies ran while one was open for 0% of the time, Pallas kernels for 17%

profile of v3, /device:TPU:264, one launch (start us, length us, event | category | flops | bytes accessed | tf_op | source)
XLA Modules:
  0.0 29.7 jit_solution(12167456415530075235)
XLA Ops:
  0.0 0.0 copy-start
  0.0 0.0 copy-start.1
  0.0 0.0 copy-start.2
  0.0 0.0 copy-start.3
  0.0 0.0 copy-start.4
  0.0 2.3 %shard_map.55 = (f32[17,16,1,128]{3,2,1,0:T(1,128)S(1)}, f32[17,16,1,128]{3,2,1,0:T(1,128)S(1)}) custom-call(s32[1,2,8]{2,1,0:T(2,128)} %active.7, f32[7,16,32,128]{3,2,1,0:T(8,128)} %g.7, f32[3,16,32,128]{3,2,1,0:T(8,128)} %vel.7, f32[16,32,128]{2,1,0:T(8,128)} %omega.7, s32[16,32,128]{2,1,0:T(8,128)} %solid.7), custom_call_target="tpu_custom_call" | custom-call | flops 1048576 | bytes 4194304 | tf_op jit(solution)/shard_map/pallas_call | solution.py:464
  2.3 3.5 %collective-permute-start = (f32[17,16,1,128]{3,2,1,0:T(1,128)S(1)}, f32[17,16,1,128]{3,2,1,0:T(1,128)S(1)}, u32[]{:S(2)}, u32[]{:S(2)}) collective-permute-start(f32[17,16,1,128]{3,2,1,0:T(1,128)S(1)} %get-tuple-element.16), channel_id=1, source_target_pairs={{1,2},{2,1},{5,6},{6,5},{9,10},{10,9},{13,14},{14,13},{17,18},{18,... | collective-permute-start | bytes 417800 | tf_op jit(solution)/shard_map/ppermute | solution.py:439
  5.8 5.8 %all-gather = f32[34,16,1,128]{3,1,2,0:T(8,128)S(1)} all-gather(f32[17,16,1,128]{3,1,2,0:T(8,128)S(1)} %bitcast.7), channel_id=2, replica_groups={{0,1},{2,3},{4,5},{6,7},{8,9},{10,11},{12,13},{14,15},{16,17},{18,19},{..., dimensions={0}, use_global_device_ids=true | all-gather | bytes 417792 | tf_op jit(solution)/shard_map/all_gather | solution.py:474
  11.6 0.0 collective-permute-done.rd
  11.6 0.0 copy-done
  11.6 0.0 copy-done.1
  11.6 0.0 copy-done.2
  11.6 0.0 copy-done.3
  11.7 0.0 copy-done.4
  11.7 0.4 %shard_map.56 = (f32[9,40,128]{2,1,0:T(8,128)S(1)}, f32[4,4,40,128]{3,2,1,0:T(8,128)S(1)}, f32[4,6,40,128]{3,2,1,0:T(8,128)S(1)}) custom-call(s32[1,2,8]{2,1,0:T(2,128)S(1)} %copy-done.4, f32[7,16,32,128]{3,2,1,0:T(8,128)S(1)} %copy-done, f32[3,16,32,128]{3,2,1,0:T(8,128)S(1)} %copy-done.1, f32[16,32,128]{2,1,0:T(8,128)S(1)} %copy-done.2, ...), custom_call_target="tpu_custom_call" | custom-call | flops 1048576 | bytes 4194304 | tf_op jit(solution)/shard_map/pallas_call | solution.py:477
  12.1 5.5 %collective-permute-start.1 = (f32[9,40,128]{2,1,0:T(8,128)S(1)}, f32[9,40,128]{2,1,0:T(8,128)S(1)}, u32[]{:S(2)}, u32[]{:S(2)}) collective-permute-start(f32[9,40,128]{2,1,0:T(8,128)S(1)} %get-tuple-element.17.rest_0_.mine), channel_id=1, source_target_pairs={{4,8},{8,4},{12,16},{16,12},{20,24},{24,20},{28,32},{32,28},{36,40... | collective-permute-start | bytes 552968 | tf_op jit(solution)/shard_map/ppermute | solution.py:439
  17.6 0.4 %shard_map.58 = (f32[9,40,128]{2,1,0:T(8,128)S(1)}, f32[4,4,40,128]{3,2,1,0:T(8,128)S(1)}, f32[4,6,40,128]{3,2,1,0:T(8,128)S(1)}) custom-call(s32[1,2,8]{2,1,0:T(2,128)S(1)} %copy-done.4, f32[7,16,32,128]{3,2,1,0:T(8,128)S(1)} %copy-done, f32[3,16,32,128]{3,2,1,0:T(8,128)S(1)} %copy-done.1, f32[16,32,128]{2,1,0:T(8,128)S(1)} %copy-done.2, ...), custom_call_target="tpu_custom_call" | custom-call | flops 1048576 | bytes 4194304 | tf_op jit(solution)/shard_map/pallas_call | solution.py:477
  18.0 3.6 %shard_map.57 = (f32[7,16,32,128]{3,2,1,0:T(8,128)}, f32[7,8,32,128]{3,2,1,0:T(8,128)S(1)}) custom-call(s32[1,2,8]{2,1,0:T(2,128)S(1)} %copy-done.4, f32[7,16,32,128]{3,2,1,0:T(8,128)S(1)} %copy-done, f32[3,16,32,128]{3,2,1,0:T(8,128)S(1)} %copy-done.1, f32[16,32,128]{2,1,0:T(8,128)S(1)} %copy-done.2, s32[16,32,128]{2,1,0:T(8,128)S(1)} %copy-done.3, ...), custom_call_target="tpu_custom_call" | custom-call | flops 16777216 | bytes 4194304 | tf_op jit(solution)/shard_map/pallas_call | solution.py:489
  21.7 2.1 %all-gather.1 = f32[18,40,128]{2,1,0:T(8,128)S(1)} all-gather(f32[9,40,128]{2,1,0:T(8,128)S(1)} %get-tuple-element.21.mine), channel_id=3, replica_groups={{0,4},{8,12},{16,20},{24,28},{32,36},{40,44},{48,52},{56,60},{64,68},{7..., dimensions={0}, use_global_device_ids=true | all-gather | bytes 552960 | tf_op jit(solution)/shard_map/all_gather | solution.py:508
  23.7 1.1 %shard_map.59.base = f32[7,16,32,128]{3,2,1,0:T(8,128)} custom-call(f32[9,40,128]{2,1,0:T(8,128)S(1)} %get-tuple-element.21.mine, f32[2,9,40,128]{3,2,1,0:T(8,128)S(1)} %bitcast.6, f32[4,4,40,128]{3,2,1,0:T(8,128)S(1)} %get-tuple-element.22.st, f32[4,6,40,128]{3,2,1,0:T(8,128)S(1)} %get-tuple-element.23.own, ...), custom_call_target="tpu_custom_call", output_to_operand_aliasing={{}: (5, {})} | custom-call | flops 1048576 | bytes 4194304 | tf_op jit(solution)/shard_map/pallas_call | solution.py:511
  24.8 3.8 %collective-permute-done.1.got = f32[9,40,128]{2,1,0:T(8,128)S(1)} collective-permute-done((f32[9,40,128]{2,1,0:T(8,128)S(1)}, f32[9,40,128]{2,1,0:T(8,128)S(1)}, u32[]{:S(2)}, u32[]{:S(2)}) %collective-permute-start.1) | collective-permute-done | bytes 184352 | tf_op jit(solution)/shard_map/ppermute | solution.py:439
  28.6 1.1 %shard_map.60 = f32[7,16,32,128]{3,2,1,0:T(8,128)} custom-call(f32[9,40,128]{2,1,0:T(8,128)S(1)} %get-tuple-element.17.rest_0_.mine, f32[9,40,128]{2,1,0:T(8,128)S(1)} %collective-permute-done.1.got, f32[4,4,40,128]{3,2,1,0:T(8,128)S(1)} %get-tuple-element.18.st, f32[4,6,40,128]{3,2,1,0:T(8,128)S(1)} %get-tuple-element.19.own, ...), custom_call_target="tpu_custom_call", output_to_operand_aliasing={{}: (5, {})} | custom-call | flops 1048576 | bytes 4194304 | tf_op jit(solution)/shard_map/pallas_call | solution.py:511
Async XLA Ops:
  0.0 11.6 %copy-start = (f32[7,16,32,128]{3,2,1,0:T(8,128)S(1)}, f32[7,16,32,128]{3,2,1,0:T(8,128)}, u32[]{:S(2)}) copy-start(f32[7,16,32,128]{3,2,1,0:T(8,128)} %g.7) | copy-start | bytes 5505028
  0.0 11.6 %copy-start.1 = (f32[3,16,32,128]{3,2,1,0:T(8,128)S(1)}, f32[3,16,32,128]{3,2,1,0:T(8,128)}, u32[]{:S(2)}) copy-start(f32[3,16,32,128]{3,2,1,0:T(8,128)} %vel.7) | copy-start | bytes 2359300
  0.0 11.6 %copy-start.2 = (f32[16,32,128]{2,1,0:T(8,128)S(1)}, f32[16,32,128]{2,1,0:T(8,128)}, u32[]{:S(2)}) copy-start(f32[16,32,128]{2,1,0:T(8,128)} %omega.7) | copy-start | bytes 786436
  0.0 11.6 %copy-start.3 = (s32[16,32,128]{2,1,0:T(8,128)S(1)}, s32[16,32,128]{2,1,0:T(8,128)}, u32[]{:S(2)}) copy-start(s32[16,32,128]{2,1,0:T(8,128)} %solid.7) | copy-start | bytes 786436
  0.0 11.6 %copy-start.4 = (s32[1,2,8]{2,1,0:T(2,128)S(1)}, s32[1,2,8]{2,1,0:T(2,128)}, u32[]{:S(2)}) copy-start(s32[1,2,8]{2,1,0:T(2,128)} %active.7) | copy-start | bytes 196
  2.3 9.3 %collective-permute-start = (f32[17,16,1,128]{3,2,1,0:T(1,128)S(1)}, f32[17,16,1,128]{3,2,1,0:T(1,128)S(1)}, u32[]{:S(2)}, u32[]{:S(2)}) collective-permute-start(f32[17,16,1,128]{3,2,1,0:T(1,128)S(1)} %get-tuple-element.16), channel_id=1, source_target_pairs={{1,2},{2,1},{5,6},{6,5},{9,10},{10,9},{13,14},{14,13},{17,18},{18,... | collective-permute-start | bytes 417800 | tf_op jit(solution)/shard_map/ppermute | solution.py:439
  12.1 16.5 %collective-permute-start.1 = (f32[9,40,128]{2,1,0:T(8,128)S(1)}, f32[9,40,128]{2,1,0:T(8,128)S(1)}, u32[]{:S(2)}, u32[]{:S(2)}) collective-permute-start(f32[9,40,128]{2,1,0:T(8,128)S(1)} %get-tuple-element.17.rest_0_.mine), channel_id=1, source_target_pairs={{4,8},{8,4},{12,16},{16,12},{20,24},{24,20},{28,32},{32,28},{36,40... | collective-permute-start | bytes 552968 | tf_op jit(solution)/shard_map/ppermute | solution.py:439

commit v4 on v3

--- a/solution.py
+++ b/solution.py
@@ -15,6 +15,7 @@
 CORNER = FIELDS + 4
 ROWS = CORNER + 2
 PARTS = 9
+SHARED = ((7, 2, 2), (0, 8, 2), (1, 4, 4), (5, 6, 4))
 F32 = jnp.float32
 MIB = 1 << 20
 
@@ -97,10 +98,15 @@
     nx, ny = omega.shape[0], omega.shape[1]
     copies = []
     for side in range(2):
-        row = (ny - TILE) * side
+        row = (ny - TILE // 2) * side
+        half = pl.ds(TILE // 2 * side, TILE // 2)
         for n, (src, dst) in enumerate(((solid, sb), (omega, ob), (vel, vb), (g, gb))):
-            window = src.at[:, :, pl.ds(row, TILE), :] if len(src.shape) == 4 else src.at[:, pl.ds(row, TILE), :]
-            copies.append(pltpu.make_async_copy(window, dst.at[side], sem.at[side, n]))
+            at = pl.ds(row, TILE // 2)
+            if len(src.shape) == 4:
+                window, into = src.at[:, :, at, :], dst.at[side, :, :, half, :]
+            else:
+                window, into = src.at[:, at, :], dst.at[side, :, half, :]
+            copies.append(pltpu.make_async_copy(window, into, sem.at[side, n]))
     copies.append(pltpu.make_async_copy(active, ab, sem.at[2, 0]))
     for copy in reversed(copies):
         copy.start()
@@ -231,7 +237,7 @@
 
 
 def face(which, active, g, vel, omega, solid, rc, rd, *rest):
-    msg, st, fl, work = rest[-4:]
+    msg, flux, st, fl, work = rest[-5:]
     y_even, x_even = even_index("gy"), even_index("gx")
     rc = rc.at[jnp.where(y_even, 1, 0)]
     nx, ny = omega.shape[0], omega.shape[1]
@@ -260,12 +266,8 @@
         gather_plane(where[p], acts, g, vel, omega, solid, halo, lambda c: work.at[0, c, p] if c < 7 else st.at[c - 7, p], (right, sign))
         write_flags(st.at[3, p], fl.at[p])
     last = slice(ny, ny + TILE)
-    msg[0, 0:ny] = work[0, 2, 0, 0:ny]
-    msg[0, last] = placed(placed(work[0, 2, 0, last], rows(corner, 12), 1), rows(corner, 14), 2)
-    msg[4] = st[0, 0] * sign
-    for c in range(1, 4):
-        msg[4 + c] = st[c, 0]
-    msg[8] = st[3, 1] * (0.125 + st[0, 1])
+    flux[0, 0:ny] = work[0, 2, 0, 0:ny]
+    flux[0, last] = placed(placed(work[0, 2, 0, last], rows(corner, 12), 1), rows(corner, 14), 2)
     for t in range(1, 4):
         old, new = (t - 1) % 2, t % 2
         for p in range(4 - t):
@@ -282,13 +284,45 @@
                 if t == 1 and r == last:
                     with_flux(out, h, rows, t, where[p])
                 if p == 0:
-                    msg[t, r] = placed(out[2], rows(corner, 13), 1) if t == 1 and r == last else out[2]
+                    flux[t, r] = placed(out[2], rows(corner, 13), 1) if t == 1 and r == last else out[2]
                 if t < 3:
                     for c in range(7):
                         work[new, c, p, r] = out[c]
 
             gs = [work.at[old, c, p] for c in range(7)]
             advance(tiles, gs, pull_1, pull_2, [st.at[c, p] for c in range(3)], st.at[3, p], fl.at[p], put)
+
+    def part(k, r):
+        if k < 4:
+            return flux[k, r]
+        if k < 8:
+            return st[0, 0, r] * sign if k == 4 else st[k - 4, 0, r]
+        return st[3, 1, r] * (0.125 + st[0, 1, r])
+
+    for k in range(PARTS):
+        for i in range(ny // TILE):
+            msg[k * (ny // TILE) + i] = part(k, slice(TILE * i, TILE * i + TILE))
+    for n, (one, two, width) in enumerate(SHARED):
+        msg[PARTS * (ny // TILE) + n] = between(part(two, last), part(one, last), width)
+
+
+def between(two, one, width):
+    sub = lax.broadcasted_iota(jnp.int32, (TILE, 128), 0)
+    middle = (sub >= (TILE - width) // 2) & (sub < (TILE + width) // 2)
+    return jnp.where(middle, pltpu.roll(two, TILE // 2, 0), one)
+
+
+def unpacked(msg, parts):
+    tiles = parts.shape[1] // TILE - 1
+    last = slice(tiles * TILE, tiles * TILE + TILE)
+    for k in range(PARTS):
+        for i in range(tiles):
+            parts[k, TILE * i:TILE * i + TILE] = msg[k * tiles + i]
+    for n, (one, two, _) in enumerate(SHARED):
+        tile = msg[PARTS * tiles + n]
+        parts[one, last] = tile
+        parts[two, last] = pltpu.roll(tile, TILE // 2, 0)
+    parts[3, last] = jnp.zeros((TILE, 128), F32)
 
 
 def interior(active, g, vel, omega, solid, rc, rd, out, near, ping, pong, stat, fl, mid, sem):
@@ -368,12 +402,12 @@
             store.wait()
 
 
-def respond(which, mine, got, st, own, near, base, out, work, flags, hu1, done, sem):
+def respond(which, mine, got, st, own, near, base, out, work, flags, hu1, theirs, done, sem):
     nx, ny = out.shape[1], out.shape[2]
     tiles = work.shape[3] // TILE
     right = even_index("gx") if which == 0 else jnp.logical_not(even_index("gx"))
     sign = jnp.where(right, 1.0, -1.0).astype(F32)
-    theirs = got.at[jnp.where(right, 1, 0)] if which == 0 else got
+    unpacked(got.at[jnp.where(right, 1, 0)] if which == 0 else got, theirs)
     hu1[...] = theirs[4] * sign
     hu = {1: [hu1, theirs.at[5], theirs.at[6]]}
     a = {1: theirs.at[7]}
@@ -476,15 +510,15 @@
     def message(which, *after):
         return call(
             functools.partial(face, which),
-            (f32(PARTS, rows, nz), f32(4, 4, rows, nz), f32(4, 6, rows, nz)),
+            (f32(PARTS * (ny // TILE) + len(SHARED), TILE, nz), f32(4, rows, nz), f32(4, 4, rows, nz), f32(4, 6, rows, nz)),
             [VM, VM, VM, VM, VM, VM, VM] + [HBM] * len(after),
-            (VM, VM, VM),
+            (VM, VM, VM, VM),
             [vm((2, 7, 4, rows, nz), F32)],
             24,
             1 << 20,
         )(active, sensitivity, velocity, omega, solid, rec_c, rec_d, *after)
 
-    msg_b, st_b, fl_b = message(1)
+    msg_b, flux_b, st_b, fl_b = message(1)
     rec_b = pair_up(msg_b, "gx", 1)
     base, near = call(
         interior,
@@ -503,7 +537,7 @@
         1 << 24,
     )(active, sensitivity, velocity, omega, solid, rec_c, rec_d)
 
-    msg_a, st_a, fl_a = message(0, msg_b)
+    msg_a, flux_a, st_a, fl_a = message(0, flux_b)
     pairs = [[i, i + 1] for i in range(0, lax.axis_size("gx"), 2)]
     rec_a = lax.all_gather(msg_a, "gx", axis_index_groups=pairs)
 
@@ -513,14 +547,14 @@
             f32(7, nx, ny, nz),
             [VM] * 5 + [HBM],
             HBM,
-            [vm((2, 7, 6, rows, nz), F32), vm((2, 6, rows, nz), F32), vm((rows, nz), F32), vm((4, 7, ny, nz), F32), dma((4,))],
+            [vm((2, 7, 6, rows, nz), F32), vm((2, 6, rows, nz), F32), vm((rows, nz), F32), vm((PARTS, rows, nz), F32), vm((4, 7, ny, nz), F32), dma((4,))],
             24,
             1 << 20,
             input_output_aliases={5: 0},
         )(mine, theirs, st, fl, near, base)
 
-    base = corrected(0, msg_a, rec_a, st_a, fl_a, base)
-    return corrected(1, msg_b, rec_b, st_b, fl_b, base)
+    base = corrected(0, flux_a, rec_a, st_a, fl_a, base)
+    return corrected(1, flux_b, rec_b, st_b, fl_b, base)
 
 
 def solution(mesh):

time: 29.9 us -> 29.3 us (0.980)
  waiting for transfers between devices: 3.83 us -> 3.44 us
    ppermute x2, waiting for transfers between devices: 3.83 us -> 3.44 us  [pair_up(): return lax.ppermute(x, axis, pairs)]
  transfers between devices with their start and end apart: 2 -> 2, of which waited for: 1 -> 1; matrix products, arithmetic and copies ran while one was open for 0% -> 0% of each run, Pallas kernels for 17% -> 18%
where the time goes in v4:
time: 29.3 us; the launch traced here: 29.1 us
  starting transfers between devices  8.95 us (31%)
  Pallas kernels  8.75 us (30%)
  blocking collectives  7.85 us (27%)
  waiting for transfers between devices  3.44 us (12%)
    ppermute x2, starting transfers between devices, pair_up(): return lax.ppermute(x, axis, pairs)  8.95 us
    all_gather x1, blocking collectives, on_device(): lax.all_gather(msg_c, 'gy', axis_index_groups=[[i, i + 1] for i in range(...  5.81 us
    pallas_call x1, Pallas kernels, on_device(): call(interior, (f32(7, nx, ny, nz), f32(7, 8, ny, nz)), [VM, VM, VM, VM,...  3.64 us
    ppermute x2, waiting for transfers between devices, pair_up(): return lax.ppermute(x, axis, pairs)  3.44 us
    pallas_call x1, Pallas kernels, on_device(): call(pack_rows, (f32(ROWS, nx, 1, nz),) * 2, [HBM, HBM, HBM, HBM, HBM], (...  2.13 us
    pallas_call x2, Pallas kernels, corrected(): call(functools.partial(respond, which), f32(7, nx, ny, nz), [VM] * 5 + [H...  2.11 us
    all_gather x1, blocking collectives, on_device(): rec_a = lax.all_gather(msg_a, 'gx', axis_index_groups=pairs)  2.04 us
    pallas_call x2, Pallas kernels, message(): call(functools.partial(face, which), (f32(PARTS * (ny // TILE) + len(SHAR...  0.87 us
  transfers between devices with their start and end apart: 2, of which 1 were waited for; matrix products, arithmetic and copies ran while one was open for 0% of the time, Pallas kernels for 18%

profile of v4, /device:TPU:264, one launch (start us, length us, event | category | flops | bytes accessed | tf_op | source)
XLA Modules:
  0.0 29.1 jit_solution(3225921672002627411)
XLA Ops:
  0.0 0.0 copy-start.4
  0.0 0.0 copy-start.3
  0.0 0.0 copy-start.2
  0.0 0.0 copy-start.1
  0.0 0.0 copy-start
  0.0 2.1 %shard_map.55 = (f32[17,16,1,128]{3,2,1,0:T(1,128)S(1)}, f32[17,16,1,128]{3,2,1,0:T(1,128)S(1)}) custom-call(s32[1,2,8]{2,1,0:T(2,128)} %active.7, f32[7,16,32,128]{3,2,1,0:T(8,128)} %g.7, f32[3,16,32,128]{3,2,1,0:T(8,128)} %vel.7, f32[16,32,128]{2,1,0:T(8,128)} %omega.7, s32[16,32,128]{2,1,0:T(8,128)} %solid.7), custom_call_target="tpu_custom_call" | custom-call | flops 1048576 | bytes 4194304 | tf_op jit(solution)/shard_map/pallas_call | solution.py:498
  2.2 3.5 %collective-permute-start = (f32[17,16,1,128]{3,2,1,0:T(1,128)S(1)}, f32[17,16,1,128]{3,2,1,0:T(1,128)S(1)}, u32[]{:S(2)}, u32[]{:S(2)}) collective-permute-start(f32[17,16,1,128]{3,2,1,0:T(1,128)S(1)} %get-tuple-element.18), channel_id=1, source_target_pairs={{1,2},{2,1},{5,6},{6,5},{9,10},{10,9},{13,14},{14,13},{17,18},{18,... | collective-permute-start | bytes 417800 | tf_op jit(solution)/shard_map/ppermute | solution.py:473
  5.7 5.8 %all-gather = f32[34,16,1,128]{3,1,2,0:T(8,128)S(1)} all-gather(f32[17,16,1,128]{3,1,2,0:T(8,128)S(1)} %bitcast.7), channel_id=2, replica_groups={{0,1},{2,3},{4,5},{6,7},{8,9},{10,11},{12,13},{14,15},{16,17},{18,19},{..., dimensions={0}, use_global_device_ids=true | all-gather | bytes 417792 | tf_op jit(solution)/shard_map/all_gather | solution.py:508
  11.5 0.0 collective-permute-done.rd
  11.5 0.0 copy-done.4
  11.5 0.0 copy-done.3
  11.5 0.0 copy-done.2
  11.5 0.0 copy-done.1
  11.5 0.0 copy-done
  11.5 0.4 %shard_map.56 = (f32[40,8,128]{2,1,0:T(8,128)S(1)}, f32[4,40,128]{2,1,0:T(8,128)S(1)}, f32[4,4,40,128]{3,2,1,0:T(8,128)S(1)}, f32[4,6,40,128]{3,2,1,0:T(8,128)S(1)}) custom-call(s32[1,2,8]{2,1,0:T(2,128)S(1)} %copy-done.4, f32[7,16,32,128]{3,2,1,0:T(8,128)S(1)} %copy-done, f32[3,16,32,128]{3,2,1,0:T(8,128)S(1)} %copy-done.1, f32[16,32,128]{2,1,0:T(8,128)S(1)} %copy-done.2, ...), custom_call_target="tpu_custom_call" | custom-call | flops 1048576 | bytes 4194304 | tf_op jit(solution)/shard_map/pallas_call | solution.py:511
  12.0 5.5 %collective-permute-start.1 = (f32[40,8,128]{2,1,0:T(8,128)S(1)}, f32[40,8,128]{2,1,0:T(8,128)S(1)}, u32[]{:S(2)}, u32[]{:S(2)}) collective-permute-start(f32[40,8,128]{2,1,0:T(8,128)S(1)} %get-tuple-element.20), channel_id=1, source_target_pairs={{4,8},{8,4},{12,16},{16,12},{20,24},{24,20},{28,32},{32,28},{36,40... | collective-permute-start | bytes 491528 | tf_op jit(solution)/shard_map/ppermute | solution.py:473
  17.4 0.4 %shard_map.58 = (f32[40,8,128]{2,1,0:T(8,128)S(1)}, f32[4,40,128]{2,1,0:T(8,128)S(1)}, f32[4,4,40,128]{3,2,1,0:T(8,128)S(1)}, f32[4,6,40,128]{3,2,1,0:T(8,128)S(1)}) custom-call(s32[1,2,8]{2,1,0:T(2,128)S(1)} %copy-done.4, f32[7,16,32,128]{3,2,1,0:T(8,128)S(1)} %copy-done, f32[3,16,32,128]{3,2,1,0:T(8,128)S(1)} %copy-done.1, f32[16,32,128]{2,1,0:T(8,128)S(1)} %copy-done.2, ...), custom_call_target="tpu_custom_call" | custom-call | flops 1048576 | bytes 4194304 | tf_op jit(solution)/shard_map/pallas_call | solution.py:511
  17.9 3.6 %shard_map.57 = (f32[7,16,32,128]{3,2,1,0:T(8,128)}, f32[7,8,32,128]{3,2,1,0:T(8,128)S(1)}) custom-call(s32[1,2,8]{2,1,0:T(2,128)S(1)} %copy-done.4, f32[7,16,32,128]{3,2,1,0:T(8,128)S(1)} %copy-done, f32[3,16,32,128]{3,2,1,0:T(8,128)S(1)} %copy-done.1, f32[16,32,128]{2,1,0:T(8,128)S(1)} %copy-done.2, s32[16,32,128]{2,1,0:T(8,128)S(1)} %copy-done.3, ...), custom_call_target="tpu_custom_call" | custom-call | flops 16777216 | bytes 4194304 | tf_op jit(solution)/shard_map/pallas_call | solution.py:523
  21.5 2.0 %all-gather.1 = f32[80,8,128]{2,1,0:T(8,128)S(1)} all-gather(f32[40,8,128]{2,1,0:T(8,128)S(1)} %get-tuple-element.25), channel_id=3, replica_groups={{0,4},{8,12},{16,20},{24,28},{32,36},{40,44},{48,52},{56,60},{64,68},{7..., dimensions={0}, use_global_device_ids=true | all-gather | bytes 491520 | tf_op jit(solution)/shard_map/all_gather | solution.py:542
  23.6 1.1 %shard_map.59.base = f32[7,16,32,128]{3,2,1,0:T(8,128)} custom-call(f32[4,40,128]{2,1,0:T(8,128)S(1)} %get-tuple-element.24.mine, f32[2,40,8,128]{3,2,1,0:T(8,128)S(1)} %bitcast.6, f32[4,4,40,128]{3,2,1,0:T(8,128)S(1)} %get-tuple-element.26.st, f32[4,6,40,128]{3,2,1,0:T(8,128)S(1)} %get-tuple-element.27.own, ...), custom_call_target="tpu_custom_call", output_to_operand_aliasing={{}: (5, {})} | custom-call | flops 1048576 | bytes 4194304 | tf_op jit(solution)/shard_map/pallas_call | solution.py:545
  24.6 3.4 %collective-permute-done.1.got = f32[40,8,128]{2,1,0:T(8,128)S(1)} collective-permute-done((f32[40,8,128]{2,1,0:T(8,128)S(1)}, f32[40,8,128]{2,1,0:T(8,128)S(1)}, u32[]{:S(2)}, u32[]{:S(2)}) %collective-permute-start.1) | collective-permute-done | bytes 163872 | tf_op jit(solution)/shard_map/ppermute | solution.py:473
  28.1 1.1 %shard_map.60 = f32[7,16,32,128]{3,2,1,0:T(8,128)} custom-call(f32[4,40,128]{2,1,0:T(8,128)S(1)} %get-tuple-element.19.rest_0_.mine, f32[40,8,128]{2,1,0:T(8,128)S(1)} %collective-permute-done.1.got, f32[4,4,40,128]{3,2,1,0:T(8,128)S(1)} %get-tuple-element.21.st, f32[4,6,40,128]{3,2,1,0:T(8,128)S(1)} %get-tuple-element.22.own, ...), custom_call_target="tpu_custom_call", output_to_operand_aliasing={{}: (5, {})} | custom-call | flops 1048576 | bytes 4194304 | tf_op jit(solution)/shard_map/pallas_call | solution.py:545
Async XLA Ops:
  0.0 11.5 %copy-start.4 = (s32[1,2,8]{2,1,0:T(2,128)S(1)}, s32[1,2,8]{2,1,0:T(2,128)}, u32[]{:S(2)}) copy-start(s32[1,2,8]{2,1,0:T(2,128)} %active.7) | copy-start | bytes 196
  0.0 11.5 %copy-start.3 = (s32[16,32,128]{2,1,0:T(8,128)S(1)}, s32[16,32,128]{2,1,0:T(8,128)}, u32[]{:S(2)}) copy-start(s32[16,32,128]{2,1,0:T(8,128)} %solid.7) | copy-start | bytes 786436
  0.0 11.5 %copy-start.2 = (f32[16,32,128]{2,1,0:T(8,128)S(1)}, f32[16,32,128]{2,1,0:T(8,128)}, u32[]{:S(2)}) copy-start(f32[16,32,128]{2,1,0:T(8,128)} %omega.7) | copy-start | bytes 786436
  0.0 11.5 %copy-start.1 = (f32[3,16,32,128]{3,2,1,0:T(8,128)S(1)}, f32[3,16,32,128]{3,2,1,0:T(8,128)}, u32[]{:S(2)}) copy-start(f32[3,16,32,128]{3,2,1,0:T(8,128)} %vel.7) | copy-start | bytes 2359300
  0.0 11.5 %copy-start = (f32[7,16,32,128]{3,2,1,0:T(8,128)S(1)}, f32[7,16,32,128]{3,2,1,0:T(8,128)}, u32[]{:S(2)}) copy-start(f32[7,16,32,128]{3,2,1,0:T(8,128)} %g.7) | copy-start | bytes 5505028
  2.2 9.3 %collective-permute-start = (f32[17,16,1,128]{3,2,1,0:T(1,128)S(1)}, f32[17,16,1,128]{3,2,1,0:T(1,128)S(1)}, u32[]{:S(2)}, u32[]{:S(2)}) collective-permute-start(f32[17,16,1,128]{3,2,1,0:T(1,128)S(1)} %get-tuple-element.18), channel_id=1, source_target_pairs={{1,2},{2,1},{5,6},{6,5},{9,10},{10,9},{13,14},{14,13},{17,18},{18,... | collective-permute-start | bytes 417800 | tf_op jit(solution)/shard_map/ppermute | solution.py:473
  12.0 16.1 %collective-permute-start.1 = (f32[40,8,128]{2,1,0:T(8,128)S(1)}, f32[40,8,128]{2,1,0:T(8,128)S(1)}, u32[]{:S(2)}, u32[]{:S(2)}) collective-permute-start(f32[40,8,128]{2,1,0:T(8,128)S(1)} %get-tuple-element.20), channel_id=1, source_target_pairs={{4,8},{8,4},{12,16},{16,12},{20,24},{24,20},{28,32},{32,28},{36,40... | collective-permute-start | bytes 491528 | tf_op jit(solution)/shard_map/ppermute | solution.py:473

commit v5 on v4

--- a/solution.py
+++ b/solution.py
@@ -68,7 +68,7 @@
     flags[5] = nf
 
 
-def advance(tiles, g, pull_1, pull_2, hu, a, flags, put, drop=None):
+def advance(tiles, g, pull_1, pull_2, hu, a, flags, put, drop=False):
     if g is not None:
         g3, g4 = g[3][...], g[4][...]
         up, down = rolled(g3, 1, 0), rolled(g4, -1, 0)
@@ -88,85 +88,79 @@
                 shift_z(g5, 1, 0.0) + flags[2, r] * g6,
                 shift_z(g6, -1, 0.0) + flags[3, r] * g5,
             ]
-        if drop is not None:
-            h[drop] = jnp.zeros_like(h[drop])
+        if drop:
+            low = lax.broadcasted_iota(jnp.int32, h[3].shape, 0) < TILE // 2
+            h[3], h[4] = jnp.where(low, h[3], 0.0), jnp.where(low, 0.0, h[4])
         put(r, collide(h, [one[r] for one in hu], a[r], flags[4, r]), h)
 
 
 def pack_rows(active, g, vel, omega, solid, msg_c, msg_d, gb, vb, ob, sb, ab, ping, pong, stat, fl, sem):
     is_even = even_index("gy")
     nx, ny = omega.shape[0], omega.shape[1]
+    half = TILE // 2
     copies = []
     for side in range(2):
-        row = (ny - TILE // 2) * side
-        half = pl.ds(TILE // 2 * side, TILE // 2)
+        rows, into = pl.ds((ny - half) * side, half), pl.ds(half * side, half)
         for n, (src, dst) in enumerate(((solid, sb), (omega, ob), (vel, vb), (g, gb))):
-            at = pl.ds(row, TILE // 2)
             if len(src.shape) == 4:
-                window, into = src.at[:, :, at, :], dst.at[side, :, :, half, :]
+                window = src.at[:, :, rows, :], dst.at[:, :, into, :]
             else:
-                window, into = src.at[:, at, :], dst.at[side, :, half, :]
-            copies.append(pltpu.make_async_copy(window, into, sem.at[side, n]))
+                window = src.at[:, rows, :], dst.at[:, into, :]
+            copies.append(pltpu.make_async_copy(*window, sem.at[side, n]))
     copies.append(pltpu.make_async_copy(active, ab, sem.at[2, 0]))
     for copy in reversed(copies):
         copy.start()
-    zero = jnp.zeros((TILE, 128), F32)
-    for side in range(2):
-        for x in (0, nx + 1):
-            fl[side, x, 5] = zero
-            for c in (1, 2):
-                ping[side, c, x] = zero
-                pong[side, c, x] = zero
+    shape = (TILE, 128)
+    zero = jnp.zeros(shape, F32)
+    for x in (0, nx + 1):
+        fl[x, 5] = zero
+        for c in (1, 2):
+            ping[c, x] = zero
+            pong[c, x] = zero
     copies[-1].wait()
-    acts = [lane_blocks(ab[0], (active.shape[1] - 1) * side, (TILE, 128)) for side in range(2)]
+    low = lax.broadcasted_iota(jnp.int32, shape, 0) < half
+    act = jnp.where(low, lane_blocks(ab[0], 0, shape), lane_blocks(ab[0], active.shape[1] - 1, shape))
     for copy in copies[:-1]:
         copy.wait()
 
-    def send(k, x, values, row):
-        low, high = values[0][row:row + 1], values[1][TILE - 1 - row:TILE - row]
-        msg_c[k, x] = jnp.where(is_even, high, low)
-        msg_d[k, x] = jnp.where(is_even, low, high)
+    def send(k, x, below, above, row):
+        first, last = below[row:row + 1], above[TILE - 1 - row:TILE - row]
+        msg_c[k, x] = jnp.where(is_even, last, first)
+        msg_d[k, x] = jnp.where(is_even, first, last)
 
     def build(x, _):
-        fields = []
-        for side in range(2):
-            f = ((1 - sb[side, x]) * acts[side]).astype(F32)
-            vals = [gb[side, c, x] * f for c in range(7)] + [0.5 * vb[side, c, x] for c in range(3)] + [f * ob[side, x]]
-            for c in range(FIELDS):
-                if c < 7:
-                    ping[side, c, x + 1] = vals[c]
-                else:
-                    stat[side, c - 7, x] = vals[c]
-            write_flags(stat.at[side, 3, x], fl.at[side, x + 1])
-            fields.append(vals)
+        f = ((1 - sb[x]) * act).astype(F32)
+        vals = [gb[c, x] * f for c in range(7)] + [0.5 * vb[c, x] for c in range(3)] + [f * ob[x]]
         for c in range(FIELDS):
-            send(c, x, [fields[0][c], fields[1][c]], 0)
-        send(FLUX, x, [fields[0][3], fields[1][4]], 1)
-        send(FLUX + 3, x, [fields[0][10] * (0.125 - fields[0][8]), fields[1][10] * (0.125 + fields[1][8])], 1)
+            if c < 7:
+                ping[c, x + 1] = vals[c]
+            else:
+                stat[c - 7, x] = vals[c]
+            send(c, x, vals[c], vals[c], 0)
+        write_flags(stat.at[3, x], fl.at[x + 1])
+        send(FLUX, x, vals[3], vals[4], 1)
+        send(FLUX + 3, x, vals[10] * (0.125 - vals[8]), vals[10] * (0.125 + vals[8]), 1)
         return 0
 
-    lax.fori_loop(0, nx, build, 0, unroll=16)
+    lax.fori_loop(0, nx, build, 0, unroll=nx)
 
     def step(x, t):
         old, new = (ping, pong) if t == 0 else (pong, ping)
-        fluxes = []
-        for side in range(2):
-
-            def pull_1(r, g2):
-                return old[side, 1, x + 2, r] + fl[side, x + 2, 5, r] * g2
-
-            def pull_2(r, g1):
-                return old[side, 2, x, r] + fl[side, x, 5, r] * g1
-
-            def put(r, res, h):
-                if t == 0:
-                    for c in range(7):
-                        new[side, c, x + 1, r] = res[c]
-                fluxes.append(res[3 + side])
-
-            gs = [old.at[side, c, x + 1] for c in range(7)]
-            advance(1, gs, pull_1, pull_2, [stat.at[side, c, x] for c in range(3)], stat.at[side, 3, x], fl.at[side, x + 1], put, None if t == 0 else 4 - side)
-        send(FLUX + 1 + t, x, fluxes, 1)
+
+        def pull_1(r, g2):
+            return old[1, x + 2, r] + fl[x + 2, 5, r] * g2
+
+        def pull_2(r, g1):
+            return old[2, x, r] + fl[x, 5, r] * g1
+
+        def put(r, res, h):
+            if t == 0:
+                for c in range(7):
+                    new[c, x + 1, r] = res[c]
+            send(FLUX + 1 + t, x, res[3], res[4], 1)
+
+        gs = [old.at[c, x + 1] for c in range(7)]
+        advance(1, gs, pull_1, pull_2, [stat.at[c, x] for c in range(3)], stat.at[3, x], fl.at[x + 1], put, t == 1)
 
     for t in range(2):
 
@@ -174,19 +168,19 @@
             step(x, t)
             return 0
 
-        lax.fori_loop(0, nx, plane, 0, unroll=16)
+        lax.fori_loop(0, nx, plane, 0, unroll=nx)
 
     for face in range(2):
         at = [nx - 1 if face else 0, nx - 2 if face else 1]
         for n, (p, row) in enumerate(((0, 1), (0, 2), (1, 1))):
             for c in range(4):
-                send(CORNER + face, 4 * n + c, [stat[side, c, at[p]] for side in range(2)], row)
-        for n, (buf, row) in enumerate(((None, 1), (pong, 1), (None, 2))):
-            if buf is None:
-                f = [((1 - sb[side, at[0]]) * acts[side]).astype(F32) for side in range(2)]
-                send(CORNER + face, 12 + n, [gb[side, 1 + face, at[0]] * f[side] for side in range(2)], row)
-            else:
-                send(CORNER + face, 12 + n, [buf[side, 1 + face, at[0] + 1] for side in range(2)], row)
+                plane = stat[c, at[p]]
+                send(CORNER + face, 4 * n + c, plane, plane, row)
+        start = gb[1 + face, at[0]] * ((1 - sb[at[0]]) * act).astype(F32)
+        after = pong[1 + face, at[0] + 1]
+        send(CORNER + face, 12, start, start, 1)
+        send(CORNER + face, 13, after, after, 1)
+        send(CORNER + face, 14, start, start, 2)
         msg_c[CORNER + face, 15] = zero[:1]
         msg_d[CORNER + face, 15] = zero[:1]
 
@@ -494,13 +488,13 @@
     dma = pltpu.SemaphoreType.DMA
 
     pinned = [pltpu.with_memory_space_constraint(v, pltpu.HBM) for v in (active, sensitivity, velocity, omega, solid)]
-    edge = lambda *shape: vm((2,) + shape + (TILE, nz), F32)
+    edge = lambda *shape: vm(shape + (TILE, nz), F32)
     msg_c, msg_d = call(
         pack_rows,
         (f32(ROWS, nx, 1, nz),) * 2,
         [HBM, HBM, HBM, HBM, HBM],
         (VM,) * 2,
-        [edge(7, nx), edge(3, nx), edge(nx), vm((2, nx, TILE, nz), jnp.int32), vm(active.shape, jnp.int32), edge(7, nx + 2), edge(7, nx + 2), edge(4, nx), edge(nx + 2, 6), dma((3, 4))],
+        [edge(7, nx), edge(3, nx), edge(nx), vm((nx, TILE, nz), jnp.int32), vm(active.shape, jnp.int32), edge(7, nx + 2), edge(7, nx + 2), edge(4, nx), edge(nx + 2, 6), dma((3, 4))],
         24,
         1 << 20,
     )(*pinned)

time: 29.3 us -> 29 us (0.990)
  no operation moved by 1% of the time
where the time goes in v5:
time: 29 us; the launch traced here: 28.9 us
  starting transfers between devices  8.95 us (31%)
  Pallas kernels  8.53 us (29%)
  blocking collectives  7.85 us (27%)
  waiting for transfers between devices  3.44 us (12%)
    ppermute x2, starting transfers between devices, pair_up(): return lax.ppermute(x, axis, pairs)  8.95 us
    all_gather x1, blocking collectives, on_device(): lax.all_gather(msg_c, 'gy', axis_index_groups=[[i, i + 1] for i in range(...  5.81 us
    pallas_call x1, Pallas kernels, on_device(): call(interior, (f32(7, nx, ny, nz), f32(7, 8, ny, nz)), [VM, VM, VM, VM,...  3.64 us
    ppermute x2, waiting for transfers between devices, pair_up(): return lax.ppermute(x, axis, pairs)  3.44 us
    pallas_call x2, Pallas kernels, corrected(): call(functools.partial(respond, which), f32(7, nx, ny, nz), [VM] * 5 + [H...  2.11 us
    all_gather x1, blocking collectives, on_device(): rec_a = lax.all_gather(msg_a, 'gx', axis_index_groups=pairs)  2.04 us
    pallas_call x1, Pallas kernels, on_device(): call(pack_rows, (f32(ROWS, nx, 1, nz),) * 2, [HBM, HBM, HBM, HBM, HBM], (...  1.91 us
    pallas_call x2, Pallas kernels, message(): call(functools.partial(face, which), (f32(PARTS * (ny // TILE) + len(SHAR...  0.87 us
  transfers between devices with their start and end apart: 2, of which 1 were waited for; matrix products, arithmetic and copies ran while one was open for 0% of the time, Pallas kernels for 18%

profile of v5, /device:TPU:264, one launch (start us, length us, event | category | flops | bytes accessed | tf_op | source)
XLA Modules:
  0.0 28.9 jit_solution(14573193278816939805)
XLA Ops:
  0.0 0.0 copy-start.4
  0.0 0.0 copy-start.3
  0.0 0.0 copy-start.2
  0.0 0.0 copy-start.1
  0.0 0.0 copy-start
  0.0 1.9 %shard_map.55 = (f32[17,16,1,128]{3,2,1,0:T(1,128)S(1)}, f32[17,16,1,128]{3,2,1,0:T(1,128)S(1)}) custom-call(s32[1,2,8]{2,1,0:T(2,128)} %active.7, f32[7,16,32,128]{3,2,1,0:T(8,128)} %g.7, f32[3,16,32,128]{3,2,1,0:T(8,128)} %vel.7, f32[16,32,128]{2,1,0:T(8,128)} %omega.7, s32[16,32,128]{2,1,0:T(8,128)} %solid.7), custom_call_target="tpu_custom_call" | custom-call | flops 1048576 | bytes 4194304 | tf_op jit(solution)/shard_map/pallas_call | solution.py:492
  1.9 3.5 %collective-permute-start = (f32[17,16,1,128]{3,2,1,0:T(1,128)S(1)}, f32[17,16,1,128]{3,2,1,0:T(1,128)S(1)}, u32[]{:S(2)}, u32[]{:S(2)}) collective-permute-start(f32[17,16,1,128]{3,2,1,0:T(1,128)S(1)} %get-tuple-element.18), channel_id=1, source_target_pairs={{1,2},{2,1},{5,6},{6,5},{9,10},{10,9},{13,14},{14,13},{17,18},{18,... | collective-permute-start | bytes 417800 | tf_op jit(solution)/shard_map/ppermute | solution.py:467
  5.4 5.8 %all-gather = f32[34,16,1,128]{3,1,2,0:T(8,128)S(1)} all-gather(f32[17,16,1,128]{3,1,2,0:T(8,128)S(1)} %bitcast.7), channel_id=2, replica_groups={{0,1},{2,3},{4,5},{6,7},{8,9},{10,11},{12,13},{14,15},{16,17},{18,19},{..., dimensions={0}, use_global_device_ids=true | all-gather | bytes 417792 | tf_op jit(solution)/shard_map/all_gather | solution.py:502
  11.2 0.0 collective-permute-done.rd
  11.3 0.0 copy-done.4
  11.3 0.0 copy-done.3
  11.3 0.0 copy-done.2
  11.3 0.0 copy-done.1
  11.3 0.0 copy-done
  11.3 0.4 %shard_map.56 = (f32[40,8,128]{2,1,0:T(8,128)S(1)}, f32[4,40,128]{2,1,0:T(8,128)S(1)}, f32[4,4,40,128]{3,2,1,0:T(8,128)S(1)}, f32[4,6,40,128]{3,2,1,0:T(8,128)S(1)}) custom-call(s32[1,2,8]{2,1,0:T(2,128)S(1)} %copy-done.4, f32[7,16,32,128]{3,2,1,0:T(8,128)S(1)} %copy-done, f32[3,16,32,128]{3,2,1,0:T(8,128)S(1)} %copy-done.1, f32[16,32,128]{2,1,0:T(8,128)S(1)} %copy-done.2, ...), custom_call_target="tpu_custom_call" | custom-call | flops 1048576 | bytes 4194304 | tf_op jit(solution)/shard_map/pallas_call | solution.py:505
  11.7 5.5 %collective-permute-start.1 = (f32[40,8,128]{2,1,0:T(8,128)S(1)}, f32[40,8,128]{2,1,0:T(8,128)S(1)}, u32[]{:S(2)}, u32[]{:S(2)}) collective-permute-start(f32[40,8,128]{2,1,0:T(8,128)S(1)} %get-tuple-element.20), channel_id=1, source_target_pairs={{4,8},{8,4},{12,16},{16,12},{20,24},{24,20},{28,32},{32,28},{36,40... | collective-permute-start | bytes 491528 | tf_op jit(solution)/shard_map/ppermute | solution.py:467
  17.2 0.4 %shard_map.58 = (f32[40,8,128]{2,1,0:T(8,128)S(1)}, f32[4,40,128]{2,1,0:T(8,128)S(1)}, f32[4,4,40,128]{3,2,1,0:T(8,128)S(1)}, f32[4,6,40,128]{3,2,1,0:T(8,128)S(1)}) custom-call(s32[1,2,8]{2,1,0:T(2,128)S(1)} %copy-done.4, f32[7,16,32,128]{3,2,1,0:T(8,128)S(1)} %copy-done, f32[3,16,32,128]{3,2,1,0:T(8,128)S(1)} %copy-done.1, f32[16,32,128]{2,1,0:T(8,128)S(1)} %copy-done.2, ...), custom_call_target="tpu_custom_call" | custom-call | flops 1048576 | bytes 4194304 | tf_op jit(solution)/shard_map/pallas_call | solution.py:505
  17.6 3.6 %shard_map.57 = (f32[7,16,32,128]{3,2,1,0:T(8,128)}, f32[7,8,32,128]{3,2,1,0:T(8,128)S(1)}) custom-call(s32[1,2,8]{2,1,0:T(2,128)S(1)} %copy-done.4, f32[7,16,32,128]{3,2,1,0:T(8,128)S(1)} %copy-done, f32[3,16,32,128]{3,2,1,0:T(8,128)S(1)} %copy-done.1, f32[16,32,128]{2,1,0:T(8,128)S(1)} %copy-done.2, s32[16,32,128]{2,1,0:T(8,128)S(1)} %copy-done.3, ...), custom_call_target="tpu_custom_call" | custom-call | flops 16777216 | bytes 4194304 | tf_op jit(solution)/shard_map/pallas_call | solution.py:517
  21.3 2.0 %all-gather.1 = f32[80,8,128]{2,1,0:T(8,128)S(1)} all-gather(f32[40,8,128]{2,1,0:T(8,128)S(1)} %get-tuple-element.25), channel_id=3, replica_groups={{0,4},{8,12},{16,20},{24,28},{32,36},{40,44},{48,52},{56,60},{64,68},{7..., dimensions={0}, use_global_device_ids=true | all-gather | bytes 491520 | tf_op jit(solution)/shard_map/all_gather | solution.py:536
  23.3 1.1 %shard_map.59.base = f32[7,16,32,128]{3,2,1,0:T(8,128)} custom-call(f32[4,40,128]{2,1,0:T(8,128)S(1)} %get-tuple-element.24.mine, f32[2,40,8,128]{3,2,1,0:T(8,128)S(1)} %bitcast.6, f32[4,4,40,128]{3,2,1,0:T(8,128)S(1)} %get-tuple-element.26.st, f32[4,6,40,128]{3,2,1,0:T(8,128)S(1)} %get-tuple-element.27.own, ...), custom_call_target="tpu_custom_call", output_to_operand_aliasing={{}: (5, {})} | custom-call | flops 1048576 | bytes 4194304 | tf_op jit(solution)/shard_map/pallas_call | solution.py:539
  24.4 3.4 %collective-permute-done.1.got = f32[40,8,128]{2,1,0:T(8,128)S(1)} collective-permute-done((f32[40,8,128]{2,1,0:T(8,128)S(1)}, f32[40,8,128]{2,1,0:T(8,128)S(1)}, u32[]{:S(2)}, u32[]{:S(2)}) %collective-permute-start.1) | collective-permute-done | bytes 163872 | tf_op jit(solution)/shard_map/ppermute | solution.py:467
  27.8 1.1 %shard_map.60 = f32[7,16,32,128]{3,2,1,0:T(8,128)} custom-call(f32[4,40,128]{2,1,0:T(8,128)S(1)} %get-tuple-element.19.rest_0_.mine, f32[40,8,128]{2,1,0:T(8,128)S(1)} %collective-permute-done.1.got, f32[4,4,40,128]{3,2,1,0:T(8,128)S(1)} %get-tuple-element.21.st, f32[4,6,40,128]{3,2,1,0:T(8,128)S(1)} %get-tuple-element.22.own, ...), custom_call_target="tpu_custom_call", output_to_operand_aliasing={{}: (5, {})} | custom-call | flops 1048576 | bytes 4194304 | tf_op jit(solution)/shard_map/pallas_call | solution.py:539
Async XLA Ops:
  0.0 11.3 %copy-start.4 = (s32[1,2,8]{2,1,0:T(2,128)S(1)}, s32[1,2,8]{2,1,0:T(2,128)}, u32[]{:S(2)}) copy-start(s32[1,2,8]{2,1,0:T(2,128)} %active.7) | copy-start | bytes 196
  0.0 11.3 %copy-start.3 = (s32[16,32,128]{2,1,0:T(8,128)S(1)}, s32[16,32,128]{2,1,0:T(8,128)}, u32[]{:S(2)}) copy-start(s32[16,32,128]{2,1,0:T(8,128)} %solid.7) | copy-start | bytes 786436
  0.0 11.3 %copy-start.2 = (f32[16,32,128]{2,1,0:T(8,128)S(1)}, f32[16,32,128]{2,1,0:T(8,128)}, u32[]{:S(2)}) copy-start(f32[16,32,128]{2,1,0:T(8,128)} %omega.7) | copy-start | bytes 786436
  0.0 11.3 %copy-start.1 = (f32[3,16,32,128]{3,2,1,0:T(8,128)S(1)}, f32[3,16,32,128]{3,2,1,0:T(8,128)}, u32[]{:S(2)}) copy-start(f32[3,16,32,128]{3,2,1,0:T(8,128)} %vel.7) | copy-start | bytes 2359300
  0.0 11.3 %copy-start = (f32[7,16,32,128]{3,2,1,0:T(8,128)S(1)}, f32[7,16,32,128]{3,2,1,0:T(8,128)}, u32[]{:S(2)}) copy-start(f32[7,16,32,128]{3,2,1,0:T(8,128)} %g.7) | copy-start | bytes 5505028
  1.9 9.3 %collective-permute-start = (f32[17,16,1,128]{3,2,1,0:T(1,128)S(1)}, f32[17,16,1,128]{3,2,1,0:T(1,128)S(1)}, u32[]{:S(2)}, u32[]{:S(2)}) collective-permute-start(f32[17,16,1,128]{3,2,1,0:T(1,128)S(1)} %get-tuple-element.18), channel_id=1, source_target_pairs={{1,2},{2,1},{5,6},{6,5},{9,10},{10,9},{13,14},{14,13},{17,18},{18,... | collective-permute-start | bytes 417800 | tf_op jit(solution)/shard_map/ppermute | solution.py:467
  11.7 16.1 %collective-permute-start.1 = (f32[40,8,128]{2,1,0:T(8,128)S(1)}, f32[40,8,128]{2,1,0:T(8,128)S(1)}, u32[]{:S(2)}, u32[]{:S(2)}) collective-permute-start(f32[40,8,128]{2,1,0:T(8,128)S(1)} %get-tuple-element.20), channel_id=1, source_target_pairs={{4,8},{8,4},{12,16},{16,12},{20,24},{24,20},{28,32},{32,28},{36,40... | collective-permute-start | bytes 491528 | tf_op jit(solution)/shard_map/ppermute | solution.py:467

commit v6 on v5

--- a/solution.py
+++ b/solution.py
@@ -450,6 +450,13 @@
                     real = c if c not in (1, 2) else jnp.where(right, c, 3 - c)
                     done[p, real, r] = near[real, x, r] + res[c]
 
+            if t == 0:
+                for i in range(tiles):
+                    r = slice(TILE * i, TILE * i + TILE)
+                    k, h = (1, pull_1(r, 0.0)) if q == 2 else (2, pull_2(r, 0.0))
+                    same = a[q][r] * ((0.125 + hu[q][0][r] if k == 1 else 0.125 - hu[q][0][r]) * h)
+                    put(r, [same + fl[q][4, r] * h if c == k else same for c in range(7)], None)
+                continue
             gs = [work.at[old, c, q] for c in range(7)] if q in live else None
             advance(tiles if t < ITERS - 1 else ny // TILE, gs, pull_1, pull_2, hu[q], a[q], fl[q], put)
             if t == ITERS - 1:

time: 29 us -> 29 us (level)
  no operation moved by 1% of the time
where the time goes in v6:
time: 29 us; the launch traced here: 28.9 us
  starting transfers between devices  8.95 us (31%)
  Pallas kernels  8.52 us (29%)
  blocking collectives  7.85 us (27%)
  waiting for transfers between devices  3.44 us (12%)
    ppermute x2, starting transfers between devices, pair_up(): return lax.ppermute(x, axis, pairs)  8.95 us
    all_gather x1, blocking collectives, on_device(): lax.all_gather(msg_c, 'gy', axis_index_groups=[[i, i + 1] for i in range(...  5.81 us
    pallas_call x1, Pallas kernels, on_device(): call(interior, (f32(7, nx, ny, nz), f32(7, 8, ny, nz)), [VM, VM, VM, VM,...  3.64 us
    ppermute x2, waiting for transfers between devices, pair_up(): return lax.ppermute(x, axis, pairs)  3.44 us
    pallas_call x2, Pallas kernels, corrected(): call(functools.partial(respond, which), f32(7, nx, ny, nz), [VM] * 5 + [H...  2.1 us
    all_gather x1, blocking collectives, on_device(): rec_a = lax.all_gather(msg_a, 'gx', axis_index_groups=pairs)  2.04 us
    pallas_call x1, Pallas kernels, on_device(): call(pack_rows, (f32(ROWS, nx, 1, nz),) * 2, [HBM, HBM, HBM, HBM, HBM], (...  1.91 us
    pallas_call x2, Pallas kernels, message(): call(functools.partial(face, which), (f32(PARTS * (ny // TILE) + len(SHAR...  0.87 us
  transfers between devices with their start and end apart: 2, of which 1 were waited for; matrix products, arithmetic and copies ran while one was open for 0% of the time, Pallas kernels for 18%

profile of v6, /device:TPU:264, one launch (start us, length us, event | category | flops | bytes accessed | tf_op | source)
XLA Modules:
  0.0 28.9 jit_solution(11631765577178331864)
XLA Ops:
  0.0 0.0 copy-start.4
  0.0 0.0 copy-start.3
  0.0 0.0 copy-start.2
  0.0 0.0 copy-start.1
  0.0 0.0 copy-start
  0.0 1.9 %shard_map.55 = (f32[17,16,1,128]{3,2,1,0:T(1,128)S(1)}, f32[17,16,1,128]{3,2,1,0:T(1,128)S(1)}) custom-call(s32[1,2,8]{2,1,0:T(2,128)} %active.7, f32[7,16,32,128]{3,2,1,0:T(8,128)} %g.7, f32[3,16,32,128]{3,2,1,0:T(8,128)} %vel.7, f32[16,32,128]{2,1,0:T(8,128)} %omega.7, s32[16,32,128]{2,1,0:T(8,128)} %solid.7), custom_call_target="tpu_custom_call" | custom-call | flops 1048576 | bytes 4194304 | tf_op jit(solution)/shard_map/pallas_call | solution.py:499
  1.9 3.5 %collective-permute-start = (f32[17,16,1,128]{3,2,1,0:T(1,128)S(1)}, f32[17,16,1,128]{3,2,1,0:T(1,128)S(1)}, u32[]{:S(2)}, u32[]{:S(2)}) collective-permute-start(f32[17,16,1,128]{3,2,1,0:T(1,128)S(1)} %get-tuple-element.18), channel_id=1, source_target_pairs={{1,2},{2,1},{5,6},{6,5},{9,10},{10,9},{13,14},{14,13},{17,18},{18,... | collective-permute-start | bytes 417800 | tf_op jit(solution)/shard_map/ppermute | solution.py:474
  5.4 5.8 %all-gather = f32[34,16,1,128]{3,1,2,0:T(8,128)S(1)} all-gather(f32[17,16,1,128]{3,1,2,0:T(8,128)S(1)} %bitcast.7), channel_id=2, replica_groups={{0,1},{2,3},{4,5},{6,7},{8,9},{10,11},{12,13},{14,15},{16,17},{18,19},{..., dimensions={0}, use_global_device_ids=true | all-gather | bytes 417792 | tf_op jit(solution)/shard_map/all_gather | solution.py:509
  11.2 0.0 collective-permute-done.rd
  11.3 0.0 copy-done.4
  11.3 0.0 copy-done.3
  11.3 0.0 copy-done.2
  11.3 0.0 copy-done.1
  11.3 0.0 copy-done
  11.3 0.4 %shard_map.56 = (f32[40,8,128]{2,1,0:T(8,128)S(1)}, f32[4,40,128]{2,1,0:T(8,128)S(1)}, f32[4,4,40,128]{3,2,1,0:T(8,128)S(1)}, f32[4,6,40,128]{3,2,1,0:T(8,128)S(1)}) custom-call(s32[1,2,8]{2,1,0:T(2,128)S(1)} %copy-done.4, f32[7,16,32,128]{3,2,1,0:T(8,128)S(1)} %copy-done, f32[3,16,32,128]{3,2,1,0:T(8,128)S(1)} %copy-done.1, f32[16,32,128]{2,1,0:T(8,128)S(1)} %copy-done.2, ...), custom_call_target="tpu_custom_call" | custom-call | flops 1048576 | bytes 4194304 | tf_op jit(solution)/shard_map/pallas_call | solution.py:512
  11.7 5.5 %collective-permute-start.1 = (f32[40,8,128]{2,1,0:T(8,128)S(1)}, f32[40,8,128]{2,1,0:T(8,128)S(1)}, u32[]{:S(2)}, u32[]{:S(2)}) collective-permute-start(f32[40,8,128]{2,1,0:T(8,128)S(1)} %get-tuple-element.20), channel_id=1, source_target_pairs={{4,8},{8,4},{12,16},{16,12},{20,24},{24,20},{28,32},{32,28},{36,40... | collective-permute-start | bytes 491528 | tf_op jit(solution)/shard_map/ppermute | solution.py:474
  17.2 0.4 %shard_map.58 = (f32[40,8,128]{2,1,0:T(8,128)S(1)}, f32[4,40,128]{2,1,0:T(8,128)S(1)}, f32[4,4,40,128]{3,2,1,0:T(8,128)S(1)}, f32[4,6,40,128]{3,2,1,0:T(8,128)S(1)}) custom-call(s32[1,2,8]{2,1,0:T(2,128)S(1)} %copy-done.4, f32[7,16,32,128]{3,2,1,0:T(8,128)S(1)} %copy-done, f32[3,16,32,128]{3,2,1,0:T(8,128)S(1)} %copy-done.1, f32[16,32,128]{2,1,0:T(8,128)S(1)} %copy-done.2, ...), custom_call_target="tpu_custom_call" | custom-call | flops 1048576 | bytes 4194304 | tf_op jit(solution)/shard_map/pallas_call | solution.py:512
  17.6 3.6 %shard_map.57 = (f32[7,16,32,128]{3,2,1,0:T(8,128)}, f32[7,8,32,128]{3,2,1,0:T(8,128)S(1)}) custom-call(s32[1,2,8]{2,1,0:T(2,128)S(1)} %copy-done.4, f32[7,16,32,128]{3,2,1,0:T(8,128)S(1)} %copy-done, f32[3,16,32,128]{3,2,1,0:T(8,128)S(1)} %copy-done.1, f32[16,32,128]{2,1,0:T(8,128)S(1)} %copy-done.2, s32[16,32,128]{2,1,0:T(8,128)S(1)} %copy-done.3, ...), custom_call_target="tpu_custom_call" | custom-call | flops 16777216 | bytes 4194304 | tf_op jit(solution)/shard_map/pallas_call | solution.py:524
  21.3 2.0 %all-gather.1 = f32[80,8,128]{2,1,0:T(8,128)S(1)} all-gather(f32[40,8,128]{2,1,0:T(8,128)S(1)} %get-tuple-element.25), channel_id=3, replica_groups={{0,4},{8,12},{16,20},{24,28},{32,36},{40,44},{48,52},{56,60},{64,68},{7..., dimensions={0}, use_global_device_ids=true | all-gather | bytes 491520 | tf_op jit(solution)/shard_map/all_gather | solution.py:543
  23.3 1.1 %shard_map.59.base = f32[7,16,32,128]{3,2,1,0:T(8,128)} custom-call(f32[4,40,128]{2,1,0:T(8,128)S(1)} %get-tuple-element.24.mine, f32[2,40,8,128]{3,2,1,0:T(8,128)S(1)} %bitcast.6, f32[4,4,40,128]{3,2,1,0:T(8,128)S(1)} %get-tuple-element.26.st, f32[4,6,40,128]{3,2,1,0:T(8,128)S(1)} %get-tuple-element.27.own, ...), custom_call_target="tpu_custom_call", output_to_operand_aliasing={{}: (5, {})} | custom-call | flops 1048576 | bytes 4194304 | tf_op jit(solution)/shard_map/pallas_call | solution.py:546
  24.4 3.4 %collective-permute-done.1.got = f32[40,8,128]{2,1,0:T(8,128)S(1)} collective-permute-done((f32[40,8,128]{2,1,0:T(8,128)S(1)}, f32[40,8,128]{2,1,0:T(8,128)S(1)}, u32[]{:S(2)}, u32[]{:S(2)}) %collective-permute-start.1) | collective-permute-done | bytes 163872 | tf_op jit(solution)/shard_map/ppermute | solution.py:474
  27.8 1.0 %shard_map.60 = f32[7,16,32,128]{3,2,1,0:T(8,128)} custom-call(f32[4,40,128]{2,1,0:T(8,128)S(1)} %get-tuple-element.19.rest_0_.mine, f32[40,8,128]{2,1,0:T(8,128)S(1)} %collective-permute-done.1.got, f32[4,4,40,128]{3,2,1,0:T(8,128)S(1)} %get-tuple-element.21.st, f32[4,6,40,128]{3,2,1,0:T(8,128)S(1)} %get-tuple-element.22.own, ...), custom_call_target="tpu_custom_call", output_to_operand_aliasing={{}: (5, {})} | custom-call | flops 1048576 | bytes 4194304 | tf_op jit(solution)/shard_map/pallas_call | solution.py:546
Async XLA Ops:
  0.0 11.3 %copy-start.4 = (s32[1,2,8]{2,1,0:T(2,128)S(1)}, s32[1,2,8]{2,1,0:T(2,128)}, u32[]{:S(2)}) copy-start(s32[1,2,8]{2,1,0:T(2,128)} %active.7) | copy-start | bytes 196
  0.0 11.3 %copy-start.3 = (s32[16,32,128]{2,1,0:T(8,128)S(1)}, s32[16,32,128]{2,1,0:T(8,128)}, u32[]{:S(2)}) copy-start(s32[16,32,128]{2,1,0:T(8,128)} %solid.7) | copy-start | bytes 786436
  0.0 11.3 %copy-start.2 = (f32[16,32,128]{2,1,0:T(8,128)S(1)}, f32[16,32,128]{2,1,0:T(8,128)}, u32[]{:S(2)}) copy-start(f32[16,32,128]{2,1,0:T(8,128)} %omega.7) | copy-start | bytes 786436
  0.0 11.3 %copy-start.1 = (f32[3,16,32,128]{3,2,1,0:T(8,128)S(1)}, f32[3,16,32,128]{3,2,1,0:T(8,128)}, u32[]{:S(2)}) copy-start(f32[3,16,32,128]{3,2,1,0:T(8,128)} %vel.7) | copy-start | bytes 2359300
  0.0 11.3 %copy-start = (f32[7,16,32,128]{3,2,1,0:T(8,128)S(1)}, f32[7,16,32,128]{3,2,1,0:T(8,128)}, u32[]{:S(2)}) copy-start(f32[7,16,32,128]{3,2,1,0:T(8,128)} %g.7) | copy-start | bytes 5505028
  1.9 9.3 %collective-permute-start = (f32[17,16,1,128]{3,2,1,0:T(1,128)S(1)}, f32[17,16,1,128]{3,2,1,0:T(1,128)S(1)}, u32[]{:S(2)}, u32[]{:S(2)}) collective-permute-start(f32[17,16,1,128]{3,2,1,0:T(1,128)S(1)} %get-tuple-element.18), channel_id=1, source_target_pairs={{1,2},{2,1},{5,6},{6,5},{9,10},{10,9},{13,14},{14,13},{17,18},{18,... | collective-permute-start | bytes 417800 | tf_op jit(solution)/shard_map/ppermute | solution.py:474
  11.7 16.1 %collective-permute-start.1 = (f32[40,8,128]{2,1,0:T(8,128)S(1)}, f32[40,8,128]{2,1,0:T(8,128)S(1)}, u32[]{:S(2)}, u32[]{:S(2)}) collective-permute-start(f32[40,8,128]{2,1,0:T(8,128)S(1)} %get-tuple-element.20), channel_id=1, source_target_pairs={{4,8},{8,4},{12,16},{16,12},{20,24},{24,20},{28,32},{32,28},{36,40... | collective-permute-start | bytes 491528 | tf_op jit(solution)/shard_map/ppermute | solution.py:474
